TPU v7x, 32 devices: a whole 2x2x4 slice. The times are simulated.
32 devices in a mesh: blk: 4 (over z), grp: 8 (over y, x, core).
Axes of the slice: x: 2, y: 2, z: 4, core: 2. Of those that a mesh axis runs over, the one named last changes fastest.
Arguments:
- user_prior: float32 [16384, 128], P(('blk', 'grp')), may hold values from -6 to 6
- item_factors: bfloat16 [131072, 128], P(('blk', 'grp')), may hold values from -0.1875 to 0.1875
- user_tiles: int32 [2048], P(('blk', 'grp')), may hold values from 0 to 31
- item_tiles: int32 [2048], P(('blk', 'grp')), may hold values from 0 to 1023, as said below
- counts: int32 [2048, 128, 128], P(('blk', 'grp')), may hold values from 0 to 20, as said below
Outputs:
- user_factors: float32 [16384, 128], P(('blk', 'grp'))
Inputs may be any that keep to these rules, and one draw needn't show every extreme that they name: `item_tiles`: item tile t is held by device t // 32 of blk+grp. The entries of one device name tiles of 32 different holders, exactly 2 entries for each holder that they name, in no particular order. In each device's 64 entries, those whose tile of counts has a nonzero value come before those whose tile is all zero; in every group along grp at least one device has all 64 entries of the first kind.
All inputs are finite; a program needn't handle non-finite values.
Results may differ from a plain program's by a relative error of at most 0.0003.
The roundings to bfloat16 on the way count: a program that leaves them out, or rounds other values in their place, can miss the bound.
Values may be sent and summed in bfloat16 or wider, within the bound.
No kernel may reach another device: no remote copies, remote signals or barrier semaphores. Data moves between devices by JAX's collectives and lax.ppermute only.
A program may use at most 128 MiB of HBM per device.

v0:
```python
import functools

import jax
import jax.numpy as jnp
from jax import lax
from jax.experimental import pallas as pl
from jax.experimental.pallas import tpu as pltpu
from jax.sharding import PartitionSpec as P

ITERS = 3

ALPHA = 40.0
REG = 32.0
EPS = 1e-06

FAR_CAP = 14
COUNT_CAP = 24
ITEM_CAP = 20
LOADS = 128
SPAN = 2
VMEM_GRANT = 60 * 2**20
TOGETHER = 8


def fetch_tiles(item_factors, item_tiles, pairs, tile, rank):
    n_all = lax.axis_size(("blk", "grp"))
    tiles_held = item_factors.shape[0] // tile
    slots_each = max(2, pairs // n_all)
    owner = item_tiles // tiles_held
    local_slot = item_tiles % tiles_held
    position = jnp.arange(pairs, dtype=jnp.int32)
    earlier = (owner[None, :] == owner[:, None]) & (position[None, :] < position[:, None])
    order = jnp.sum(earlier.astype(jnp.int32), axis=1)
    requests = jnp.full((n_all, slots_each), -1, jnp.int32).at[owner, order].set(local_slot)
    wanted = lax.all_to_all(requests, ("blk", "grp"), split_axis=0, concat_axis=0, tiled=True)
    held = item_factors.reshape(tiles_held, tile, rank)
    picked = jnp.take(held, jnp.maximum(wanted, 0), axis=0)
    picked = jnp.where((wanted >= 0)[:, :, None, None], picked, jnp.zeros((), picked.dtype))
    arrived = lax.all_to_all(picked, ("blk", "grp"), split_axis=0, concat_axis=0, tiled=True)
    return arrived[owner, order]


def row_sum(left, right):
    return jnp.sum(left * right, axis=1, keepdims=True)


def sweep_in_place(user_prior, item_factors, user_tiles, item_tiles, counts, live, gram_local):
    pairs = counts.shape[0]
    tile = counts.shape[1]
    rank = item_factors.shape[1]
    n_grp = lax.axis_size("grp")
    own_rows = user_prior.shape[0]
    block_rows = own_rows * n_grp
    user_blocks = block_rows // tile
    span = min(32, pairs)
    gram = lax.psum(gram_local, ("blk", "grp"))
    pair_tiles = fetch_tiles(item_factors, item_tiles, pairs, tile, rank)
    rounds = (jnp.sum(live.astype(jnp.int32)) + span - 1) // span
    tile_ids = jnp.arange(user_blocks, dtype=jnp.int32)

    def accumulate(low_tiles, with_rhs):

        def one_round(index, totals):
            start = index * span
            users = lax.dynamic_slice_in_dim(user_tiles, start, span)
            factors = lax.dynamic_slice_in_dim(pair_tiles, start, span)
            counted = lax.dynamic_slice_in_dim(counts, start, span).astype(jnp.float32)
            selector = (tile_ids[:, None] == users[None, :]).astype(jnp.float32)
            users_low = jnp.take(low_tiles, users, axis=0)
            scores = jnp.einsum(
                "bur,bir->bui", users_low, factors, preferred_element_type=jnp.float32
            )
            scaled = (ALPHA * counted * scores).astype(jnp.bfloat16)
            back = jnp.einsum("bui,bir->bur", scaled, factors, preferred_element_type=jnp.float32)
            result = [
                totals[0]
                + jnp.einsum("tb,bur->tur", selector, back, precision=lax.Precision.HIGHEST)
            ]
            if with_rhs:
                confidence = jnp.where(counted > 0, 1.0 + ALPHA * counted, 0.0).astype(jnp.bfloat16)
                pulled = jnp.einsum(
                    "bui,bir->bur", confidence, factors, preferred_element_type=jnp.float32
                )
                result.append(
                    totals[1]
                    + jnp.einsum("tb,bur->tur", selector, pulled, precision=lax.Precision.HIGHEST)
                )
            return tuple(result)

        zeros = jnp.zeros((user_blocks, tile, rank), jnp.float32)
        start_state = (zeros, zeros) if with_rhs else (zeros,)
        totals = lax.fori_loop(0, rounds, one_round, start_state)
        return tuple((total.reshape(block_rows, rank) for total in totals))

    def gram_term(vectors):
        return jnp.dot(vectors, gram, precision=lax.Precision.HIGHEST) + REG * vectors

    low = lax.all_gather(user_prior.astype(jnp.bfloat16), "grp", axis=0, tiled=True)
    pair_part, rhs_part = accumulate(low.reshape(user_blocks, tile, rank), True)
    pair_share, rhs_share = (
        lax.psum_scatter(pair_part, "grp", scatter_dimension=0, tiled=True),
        lax.psum_scatter(rhs_part, "grp", scatter_dimension=0, tiled=True),
    )
    solution = user_prior
    residual = rhs_share - (gram_term(solution) + pair_share)
    direction = residual
    norm_now = row_sum(residual, residual)
    for step in range(ITERS):
        low = lax.all_gather(direction.astype(jnp.bfloat16), "grp", axis=0, tiled=True)
        (pair_part,) = accumulate(low.reshape(user_blocks, tile, rank), False)
        image = gram_term(direction) + lax.psum_scatter(
            pair_part, "grp", scatter_dimension=0, tiled=True
        )
        alpha = norm_now / (row_sum(direction, image) + EPS)
        solution = solution + alpha * direction
        residual = residual - alpha * image
        fresh = row_sum(residual, residual)
        direction = residual + fresh / (norm_now + EPS) * direction
        norm_now = fresh
    return solution


def bits_for(n):
    return (n - 1).bit_length()


def at_source(number, row, n_sources):
    return (row << bits_for(n_sources)) + number


def move_tile(sources, at, room, place):
    bits = bits_for(len(sources))
    row = lax.shift_right_logical(at, bits)
    which = at & ((1 << bits) - 1)

    def among(lo, hi):
        if hi - lo == 1:
            room[place] = sources[lo][row]
            return
        mid = (lo + hi) // 2
        pl.when(which < mid)(lambda: among(lo, mid))
        pl.when(which >= mid)(lambda: among(mid, hi))

    among(0, len(sources))


def sweep_kernel(n_counts, plan, prior_ref, gram_ref, *refs):
    weights, factors, low, image, residual, direction = refs[-6:]
    count_pieces, item_pieces, out_ref = refs[:n_counts], refs[n_counts:-7], refs[-7]
    tile, rank = factors.shape[1:]
    rounds = plan[6, 0]

    def bring(place, carry):
        count_at = plan[3, place]
        item_at = plan[4, place]

        @pl.when(count_at > 0)
        def _():
            move_tile(count_pieces, count_at - 1, weights, place)
            move_tile(item_pieces, item_at, factors, place)

        @pl.when(count_at == 0)
        def _():
            weights[place] = jnp.zeros((tile, tile), weights.dtype)
            factors[place] = jnp.zeros((tile, rank), factors.dtype)

        return carry

    lax.fori_loop(0, rounds * (TOGETHER * SPAN), bring, 0)

    def pair_images(with_rhs):
        image[...] = jnp.zeros_like(image)
        if with_rhs:
            residual[...] = jnp.zeros_like(residual)

        def one_round(step, carry):
            shares = []
            for number in range(TOGETHER):
                chunk = step * TOGETHER + number
                rows = pl.ds(pl.multiple_of(plan[5, chunk] * tile, tile), tile)
                items = factors[pl.ds(chunk * SPAN, SPAN)].reshape(SPAN * tile, rank)
                scaled = jnp.concatenate(
                    [weights[chunk * SPAN + part].astype(jnp.float32) for part in range(SPAN)],
                    axis=1,
                )
                scores = lax.dot_general(
                    low[rows, :], items, (((1,), (1,)), ((), ())),
                    preferred_element_type=jnp.float32,
                )
                back = jnp.dot(
                    (scaled * scores).astype(jnp.bfloat16), items,
                    preferred_element_type=jnp.float32,
                )
                pulled = None
                if with_rhs:
                    confidence = jnp.where(scaled > 0, 1.0 + scaled, 0.0).astype(jnp.bfloat16)
                    pulled = jnp.dot(confidence, items, preferred_element_type=jnp.float32)
                shares.append((rows, back, pulled))
            for rows, back, pulled in shares:
                image[rows, :] += back
                if with_rhs:
                    residual[rows, :] += pulled
            return carry

        lax.fori_loop(0, rounds, one_round, 0)

    def gram_term(vectors):
        return jnp.dot(
            vectors, gram_ref[...], precision=lax.Precision.HIGHEST,
            preferred_element_type=jnp.float32,
        ) + REG * vectors

    prior = prior_ref[...]
    low[...] = prior.astype(jnp.bfloat16)
    pair_images(True)
    first = residual[...] - (gram_term(prior) + image[...])
    residual[...] = first
    direction[...] = first
    out_ref[...] = prior
    norm_now = row_sum(first, first)
    for step in range(ITERS):
        heading = direction[...]
        low[...] = heading.astype(jnp.bfloat16)
        pair_images(False)
        shown = gram_term(heading) + image[...]
        alpha = norm_now / (row_sum(heading, shown) + EPS)
        out_ref[...] += alpha * heading
        if step < ITERS - 1:
            left = residual[...] - alpha * shown
            residual[...] = left
            fresh = row_sum(left, left)
            direction[...] = left + (fresh / (norm_now + EPS)) * heading
            norm_now = fresh


def run_sweep(plan, user_prior, gram, count_pieces, item_pieces):
    own_rows, rank = user_prior.shape
    tile = count_pieces[0].shape[1]
    pieces = [*count_pieces, *item_pieces]
    vmem = pl.BlockSpec(memory_space=pltpu.VMEM)
    return pl.pallas_call(
        functools.partial(sweep_kernel, len(count_pieces)),
        out_shape=jax.ShapeDtypeStruct((own_rows, rank), jnp.float32),
        in_specs=[pl.BlockSpec(memory_space=pltpu.SMEM)] + [vmem] * (2 + len(pieces)),
        out_specs=vmem,
        scratch_shapes=[
            pltpu.VMEM((LOADS, tile, tile), jnp.bfloat16),
            pltpu.VMEM((LOADS, tile, rank), jnp.bfloat16),
            pltpu.VMEM((own_rows, rank), jnp.bfloat16),
            pltpu.VMEM((own_rows, rank), jnp.float32),
            pltpu.VMEM((own_rows, rank), jnp.float32),
            pltpu.VMEM((own_rows, rank), jnp.float32),
        ],
        compiler_params=pltpu.CompilerParams(vmem_limit_bytes=32 * 2**20),
        name="sweep",
    )(plan, user_prior, gram, *pieces)


def pack_kernel(n_sources, n_outs, jobs, table, *refs):
    sources, refs = refs[:n_sources], refs[n_sources:]
    outs, rooms, written = refs[:n_outs], refs[n_outs:-1], refs[-1]
    copies = []
    for number, (lo, hi, row, start, length, out, first) in enumerate(jobs):

        def place(spot, carry, number=number, lo=lo, hi=hi, row=row, start=start):
            move_tile(sources[lo:hi], table[row, start + spot], rooms[number], spot)
            return carry

        lax.fori_loop(0, length, place, 0, unroll=2)
        target = outs[out].at[pl.ds(first, length)]
        copies.append(pltpu.make_async_copy(rooms[number], target, written.at[number]))
        copies[-1].start()
    for copy in copies:
        copy.wait()


def pack_tiles(name, table, sources, lengths, jobs):
    anywhere = pl.BlockSpec(memory_space=pl.ANY)
    kind = sources[0].dtype
    shape = sources[0].shape[1:]
    return pl.pallas_call(
        functools.partial(pack_kernel, len(sources), len(lengths), jobs),
        out_shape=[jax.ShapeDtypeStruct((n, *shape), kind) for n in lengths],
        in_specs=[pl.BlockSpec(memory_space=pltpu.SMEM)]
        + [pl.BlockSpec(memory_space=pltpu.VMEM)] * len(sources),
        out_specs=[anywhere] * len(lengths),
        scratch_shapes=[pltpu.VMEM((job[4], *shape), kind) for job in jobs]
        + [pltpu.SemaphoreType.DMA((len(jobs),))],
        compiler_params=pltpu.CompilerParams(vmem_limit_bytes=VMEM_GRANT),
        name=name,
    )(table, *sources)


def sum_with(value, axis, bit):
    size = lax.axis_size(axis)
    return value + lax.ppermute(value, axis, [(i, i ^ bit) for i in range(size)])


def iota(rows, columns, axis):
    return lax.broadcasted_iota(jnp.int32, (rows, columns), axis)


def dot_nt(left, right):
    return lax.dot_general(
        left.astype(jnp.bfloat16), right.astype(jnp.bfloat16), (((1,), (1,)), ((), ())),
        preferred_element_type=jnp.float32,
    )


def choose(key, hit, cells, *values):
    match = hit & (key == iota(cells, key.shape[1], 0))
    row = iota(8, key.shape[1], 0)
    digits = jnp.zeros((8, key.shape[1]), jnp.int32)
    for number, value in enumerate(values):
        digits = jnp.where(row == 2 * number, value & 31, digits)
        digits = jnp.where(row == 2 * number + 1, lax.shift_right_logical(value, 5), digits)
    found = dot_nt(digits.astype(jnp.float32), match.astype(jnp.float32)).astype(jnp.int32)
    return [
        found[2 * number:2 * number + 1] + 32 * found[2 * number + 1:2 * number + 2]
        for number in range(len(values))
    ]


def route_kernel(n_grp, pairs, own_tiles, tiles_held, spot, every_ref, out_ref):
    n_blk, n_entries = every_ref.shape
    width = out_ref.shape[1]
    n_chips = n_grp // 2
    user_blocks = n_grp * own_tiles
    all_chips = n_blk * n_chips
    pad = lambda n: -(-n // 8) * 8
    my_blk, my_grp = spot[0], spot[1]
    my_chip = lax.shift_right_logical(my_grp, 1)
    my_core = my_grp & 1
    index = iota(1, n_entries, 1)
    source = lax.shift_right_logical(index, bits_for(pairs))
    from_chip = lax.shift_right_logical(source, 1)
    one_hot = lambda key, n: key == iota(pad(n), n_entries, 0)

    def fields(packed):
        user = packed & (user_blocks - 1)
        packed = lax.shift_right_logical(packed, bits_for(user_blocks))
        live = (packed & 1) == 1
        item = lax.shift_right_logical(packed, 1)
        held = item & (2 * tiles_held - 1)
        chip = lax.shift_right_logical(item, bits_for(2 * tiles_held))
        return user, live, chip, held

    ids = iota(1, 2 * tiles_held, 1)
    fewer = iota(2 * tiles_held, 2 * tiles_held, 0) > iota(2 * tiles_held, 2 * tiles_held, 1)

    def needs(live, chip, held):
        on_chip = one_hot(chip, all_chips) & live
        on_tile = one_hot(held, 2 * tiles_held)
        needed = dot_nt(on_chip.astype(jnp.float32), on_tile.astype(jnp.float32)) > 0
        return on_chip, on_tile, needed, dot_nt(needed.astype(jnp.float32), fewer.astype(jnp.float32))

    excess = jnp.zeros((1, 1), jnp.float32)
    worst = lambda loads, room: jnp.max(loads, axis=(0, 1), keepdims=True) - room
    asked = jnp.zeros((1, width), jnp.int32)
    here = my_blk * n_chips + my_chip
    chip_row = iota(pad(all_chips), 2 * tiles_held, 0)
    for blk in range(n_blk):
        user, live, chip, held = fields(every_ref[blk:blk + 1, :])
        _, _, needed, ahead = needs(live, chip, held)
        away = lax.shift_right_logical(chip_row, bits_for(n_chips)) != blk
        asks = jnp.sum((needed & away).astype(jnp.float32), axis=1, keepdims=True)
        excess = jnp.maximum(excess, worst(asks, 2 * FAR_CAP))
        to_chip = lax.shift_right_logical(user, bits_for(own_tiles) + 1)
        to = one_hot(to_chip, n_chips).astype(jnp.float32)
        for key, cap in ((from_chip, COUNT_CAP), (chip & (n_chips - 1), ITEM_CAP)):
            loads = dot_nt((one_hot(key, n_chips) & live).astype(jnp.float32), to)
            excess = jnp.maximum(excess, worst(loads, 2 * cap))
        loads = jnp.sum(
            (one_hot(user, user_blocks) & live).astype(jnp.int32), axis=1, keepdims=True
        )
        chunks = lax.shift_right_logical(loads + SPAN - 1, bits_for(SPAN)).astype(jnp.float32)
        owners = iota(pad(n_grp), pad(user_blocks), 1)
        owners = lax.shift_right_logical(owners, bits_for(own_tiles)) == iota(*owners.shape, 0)
        loads = jnp.dot(
            owners.astype(jnp.float32), jnp.broadcast_to(chunks, (chunks.shape[0], 128)),
            precision=lax.Precision.HIGHEST, preferred_element_type=jnp.float32,
        )
        excess = jnp.maximum(excess, worst(loads, LOADS // SPAN))

        mine = chip_row == here
        present = jnp.sum((needed & mine).astype(jnp.int32), axis=0, keepdims=True)
        place = jnp.sum(jnp.where(mine, ahead, 0.0), axis=0, keepdims=True).astype(jnp.int32)
        shift = (blk + n_blk - my_blk) & (n_blk - 1)
        spot_at = lax.shift_right_logical(place, 1)
        hit = (present > 0) & ((place & 1) == my_core) & (spot_at < FAR_CAP) & (shift > 0)
        value = at_source(
            lax.shift_right_logical(ids, bits_for(tiles_held)) ^ my_core, ids & (tiles_held - 1), 2
        )
        (found,) = choose((shift - 1) * FAR_CAP + spot_at, hit, width, value)
        asked = asked + found

    user, live, chip, held = fields(every_ref[pl.ds(my_blk, 1), :])
    on_chip, on_tile, _, ahead = needs(live, chip, held)
    places = jnp.dot(
        ahead.astype(jnp.bfloat16), on_tile.astype(jnp.float32).astype(jnp.bfloat16),
        preferred_element_type=jnp.float32,
    )
    far_place = jnp.sum(jnp.where(on_chip, places, 0.0), axis=0, keepdims=True).astype(jnp.int32)
    far_place = jnp.minimum(far_place, 2 * FAR_CAP - 1)
    owner = lax.shift_right_logical(user, bits_for(own_tiles))
    local_user = user & (own_tiles - 1)
    to_chip = lax.shift_right_logical(owner, 1)
    column = chip & (n_chips - 1)
    to_me = live & (owner == my_grp)
    groups = [
        one_hot(to_chip, n_chips) & (live & (from_chip == my_chip)),
        one_hot(from_chip, n_chips) & (live & (to_chip == my_chip)),
        one_hot(to_chip, n_chips) & (live & (column == my_chip)),
        one_hot(column, n_chips) & (live & (to_chip == my_chip)),
        one_hot(local_user, own_tiles) & to_me,
    ]
    before = (iota(n_entries, n_entries, 0) < iota(n_entries, n_entries, 1)).astype(jnp.float32)
    before = before.astype(jnp.bfloat16)
    ranks = []
    for marks in groups:
        earlier = jnp.dot(
            marks.astype(jnp.float32).astype(jnp.bfloat16), before,
            preferred_element_type=jnp.float32,
        )
        earlier = jnp.sum(jnp.where(marks, earlier, 0.0), axis=0, keepdims=True)
        ranks.append(earlier.astype(jnp.int32))
    counts_out, counts_back, items_out, items_back, user_rank = ranks

    half = lambda rank: lax.shift_right_logical(rank, 1)
    sent = lambda rank, cap: live & ((rank & 1) == my_core) & (half(rank) < cap)
    (out_ref[0:1, :],) = choose(
        to_chip * COUNT_CAP + half(counts_out), sent(counts_out, COUNT_CAP) & (from_chip == my_chip),
        width, at_source((source & 1) ^ my_core, index & (pairs - 1), 2),
    )
    out_ref[1:2, :] = asked
    shift = (my_blk + n_blk - lax.shift_right_logical(chip, bits_for(n_chips))) & (n_blk - 1)
    near = shift == 0
    lane = jnp.where(near, lax.shift_right_logical(held, bits_for(tiles_held)), far_place & 1)
    row = jnp.where(near, held & (tiles_held - 1), half(far_place))
    (out_ref[2:3, :],) = choose(
        (to_chip ^ my_chip) * ITEM_CAP + half(items_out),
        sent(items_out, ITEM_CAP) & (column == my_chip),
        width, at_source((lane ^ my_core) * n_blk + shift, row, 2 * n_blk),
    )

    in_tile = groups[4]
    loads = jnp.sum(in_tile.astype(jnp.int32), axis=1, keepdims=True)
    chunks = lax.shift_right_logical(loads + SPAN - 1, bits_for(SPAN)).astype(jnp.float32)
    rows = chunks.shape[0]
    ends = jnp.dot(
        (iota(rows, rows, 0) >= iota(rows, rows, 1)).astype(jnp.float32),
        jnp.broadcast_to(chunks, (rows, 128)),
        precision=lax.Precision.HIGHEST, preferred_element_type=jnp.float32,
    )
    firsts = ends[:, :1] - chunks
    room_at = jnp.sum(jnp.where(in_tile, firsts * SPAN, 0.0), axis=0, keepdims=True)
    room_at = room_at.astype(jnp.int32) + user_rank
    hit = to_me & (room_at < LOADS)
    counts_row = jnp.minimum(half(counts_back), COUNT_CAP - 1)
    items_row = jnp.minimum(half(items_back), ITEM_CAP - 1)
    count_at = at_source((counts_back & 1) ^ my_core, from_chip * COUNT_CAP + counts_row, 2)
    item_at = at_source(
        (column ^ my_chip) * 2 + ((items_back & 1) ^ my_core), items_row, 2 * n_chips
    )
    out_ref[3:4, :], out_ref[4:5, :] = choose(room_at, hit, width, count_at + 1, item_at)
    passed = (iota(rows, width, 1).astype(jnp.float32) >= ends[:, :1]) & (
        iota(rows, width, 0) < own_tiles - 1
    )
    out_ref[5:6, :] = jnp.sum(passed.astype(jnp.int32), axis=0, keepdims=True)
    total = ends[own_tiles - 1:own_tiles, :1].astype(jnp.int32)
    rounds = lax.shift_right_logical(total + TOGETHER - 1, bits_for(TOGETHER))
    rounds = jnp.minimum(rounds, LOADS // (SPAN * TOGETHER))
    copies = jnp.sum(hit.astype(jnp.int32), axis=1, keepdims=True)
    at = iota(1, width, 1)
    fits = (excess <= 0.0).astype(jnp.int32)
    head = jnp.where(at == 0, rounds, jnp.where(at == 1, copies, jnp.where(at == 2, fits, 0)))
    out_ref[6:7, :] = head
    out_ref[7:8, :] = jnp.zeros((1, width), jnp.int32)


def route(every, my_blk, my_grp, n_grp, own_tiles, tiles_held):
    n_blk, n_entries = every.shape
    n_chips = n_grp // 2
    width = max(n_chips * COUNT_CAP, (n_blk - 1) * FAR_CAP, n_chips * ITEM_CAP, LOADS)
    width = -(-width // 128) * 128
    vmem = pl.BlockSpec(memory_space=pltpu.VMEM)
    return pl.pallas_call(
        functools.partial(route_kernel, n_grp, n_entries // n_grp, own_tiles, tiles_held),
        out_shape=jax.ShapeDtypeStruct((8, width), jnp.int32),
        in_specs=[pl.BlockSpec(memory_space=pltpu.SMEM), vmem],
        out_specs=vmem,
        compiler_params=pltpu.CompilerParams(vmem_limit_bytes=16 * 2**20),
        name="route",
    )(jnp.stack([my_blk, my_grp]).astype(jnp.int32), every)


def scan_kernel(counts_ref, scaled_ref, most_ref):
    counts = counts_ref[...]
    scaled_ref[...] = (ALPHA * counts.astype(jnp.float32)).astype(jnp.bfloat16)
    most_ref[...] = jnp.max(counts, axis=1)


def scan_counts(counts):
    pairs, tile, columns = counts.shape
    block = 16
    return pl.pallas_call(
        scan_kernel,
        grid=(pairs // block,),
        out_shape=[
            jax.ShapeDtypeStruct(counts.shape, jnp.bfloat16),
            jax.ShapeDtypeStruct((pairs, columns), jnp.int32),
        ],
        in_specs=[pl.BlockSpec((block, tile, columns), lambda i: (i, 0, 0))],
        out_specs=[
            pl.BlockSpec((block, tile, columns), lambda i: (i, 0, 0)),
            pl.BlockSpec((block, columns), lambda i: (i, 0)),
        ],
        compiler_params=pltpu.CompilerParams(vmem_limit_bytes=16 * 2**20),
        name="scan_counts",
    )(counts)


def body(user_prior, item_factors, user_tiles, item_tiles, counts):
    pairs = counts.shape[0]
    tile = counts.shape[1]
    rank = item_factors.shape[1]
    n_blk = lax.axis_size("blk")
    n_grp = lax.axis_size("grp")
    n_all = n_blk * n_grp
    n_chips = n_grp // 2
    own_rows = user_prior.shape[0]
    own_tiles = own_rows // tile
    user_blocks = own_tiles * n_grp
    tiles_held = item_factors.shape[0] // tile
    my_blk = lax.axis_index("blk")
    my_grp = lax.axis_index("grp")
    my_chip = my_grp // 2
    my_core = my_grp % 2
    lanes = [[chip * 2 + core for chip in range(n_chips)] for core in range(2)]

    def swap(value):
        return lax.ppermute(value, "grp", [(i, i ^ 1) for i in range(n_grp)])

    def to_chips(value):
        return lax.all_to_all(
            value, "grp", split_axis=0, concat_axis=0, tiled=True, axis_index_groups=lanes
        )

    gram_local = lax.dot_general(
        item_factors, item_factors, (((0,), (0,)), ((), ())), preferred_element_type=jnp.float32
    )
    grp_bits, blk_bits = [[1 << n for n in range(bits_for(size))] for size in (n_grp, n_blk)]
    held = item_factors.reshape(tiles_held, tile, rank)
    held_mate = swap(held)
    scaled, column_most = scan_counts(counts)
    live = jnp.any(column_most > 0, axis=1)
    scaled_mate = swap(scaled)
    packed = (item_tiles * 2 + live.astype(jnp.int32)) * user_blocks + user_tiles
    every = lax.all_to_all(
        jnp.broadcast_to(packed, (n_all, pairs)), ("blk", "grp"),
        split_axis=0, concat_axis=0, tiled=True,
    )
    table = route(every.reshape(n_blk, n_grp * pairs), my_blk, my_grp, n_grp, own_tiles, tiles_held)
    gram = gram_local
    for bit in grp_bits[1:]:
        gram = sum_with(gram, "grp", bit)
    table, gram = lax.optimization_barrier((table, gram))

    jobs = [(0, 2, 1, shift * FAR_CAP, FAR_CAP, shift, 0) for shift in range(n_blk - 1)]
    for chip in range(n_chips):
        jobs.append((2, 4, 0, chip * COUNT_CAP, COUNT_CAP, n_blk - 1, chip * COUNT_CAP))
    lengths = [FAR_CAP] * (n_blk - 1) + [n_chips * COUNT_CAP]
    *far, counts_out = pack_tiles(
        "pack_first", table, [held, held_mate, scaled, scaled_mate], lengths, jobs
    )
    far = [
        lax.ppermute(piece, "blk", [(i, (i + 1 + shift) % n_blk) for i in range(n_blk)])
        for shift, piece in enumerate(far)
    ]
    far_mate = [swap(piece) for piece in far]
    counts_own = to_chips(counts_out)

    jobs = [(0, 2 * n_blk, 2, off * ITEM_CAP, ITEM_CAP, off, 0) for off in range(n_chips)]
    items_out = pack_tiles(
        "pack_items", table, [held, *far, held_mate, *far_mate], [ITEM_CAP] * n_chips, jobs
    )
    counts_own, gram, *items_out = lax.optimization_barrier((counts_own, gram, *items_out))
    counts_mate = swap(counts_own)
    gram = sum_with(gram, "grp", grp_bits[0])
    for bit in blk_bits:
        gram = sum_with(gram, "blk", bit)
    item_pieces = []
    for off, piece in enumerate(items_out):
        if off:
            piece = lax.ppermute(piece, "grp", [(i, i ^ (2 * off)) for i in range(n_grp)])
        if off == n_chips - 1:
            piece, gram = lax.optimization_barrier((piece, gram))
        item_pieces += [piece, swap(piece)]
    by_owner = run_sweep(table, user_prior, gram, [counts_own, counts_mate], item_pieces)

    fits = table[6, 2] > 0
    return lax.cond(
        fits, lambda done, *given: done, lambda done, *given: sweep_in_place(*given),
        by_owner, user_prior, item_factors, user_tiles, item_tiles, counts, live, gram_local,
    )


def solution(mesh):
    in_specs = (
        P(("blk", "grp"), None),
        P(("blk", "grp"), None),
        P(("blk", "grp")),
        P(("blk", "grp")),
        P(("blk", "grp"), None, None),
    )
    out_specs = P(("blk", "grp"), None)
    return jax.shard_map(body, mesh=mesh, in_specs=in_specs, out_specs=out_specs, check_vma=False)
```

profile of v0, /device:TPU:11, one launch (start us, length us, event | category | flops | bytes accessed | tf_op | source)
XLA Modules:
  0.0 149.3 jit_solution(10775511202636572926)
XLA Ops:
  6.5 3.3 %scan_counts.1 = (bf16[64,128,128]{2,1,0:T(8,128)(2,1)S(1)}, s32[64,128]{1,0:T(8,128)S(1)}) custom-call(s32[64,128,128]{2,1,0:T(8,128)} %counts_ref.1), custom_call_target="tpu_custom_call" | custom-call | tf_op jit(solution)/shard_map/scan_counts/pallas_call | solution.py:506
  9.9 0.7 collective-permute-start.3
  10.6 0.1 collective-permute-start.2
  10.7 0.5 fusion.131
  11.2 0.3 collective-permute-start
  11.5 0.1 compare_reduce_fusion
  11.6 0.6 broadcast_in_dim.41
  12.3 6.4 %all-to-all-start.2 = ((s32[32,1,64]{2,1,0:T(1,128)}), s32[32,1,64]{2,1,0:T(1,128)S(1)}, u32[]{:S(2)}, u32[]{:S(2)}) async-start(s32[32,1,64]{2,1,0:T(1,128)} %broadcast_in_dim.41), calls=%async_computation.7 | async-start | bytes 32768 | tf_op jit(solution)/shard_map/all_to_all | solution.py:559
  18.7 1.2 collective-permute-start.1
  20.0 3.3 %all-to-all-done.2 = s32[32,1,64]{2,1,0:T(1,128)S(1)} async-done(((s32[32,1,64]{2,1,0:T(1,128)}), s32[32,1,64]{2,1,0:T(1,128)S(1)}, u32[]{:S(2)}, u32[]{:S(2)}) %all-to-all-start.2) | async-done | bytes 8224 | tf_op jit(solution)/shard_map/all_to_all | solution.py:559
  23.3 0.5 broadcast.304
  23.8 0.7 reduce.3
  24.6 2.3 %route.1.table.plan = s32[8,128]{1,0:T(8,128)S(1)} custom-call(s32[2]{0:T(128)S(1)} %pad_add_fusion.spot, s32[4,512]{1,0:T(4,128)S(1)} %reshape.144.every_ref), custom_call_target="tpu_custom_call" | custom-call | tf_op jit(solution)/shard_map/route/pallas_call | solution.py:487
  27.0 0.6 copy-done.2
  27.6 0.6 add.202
  28.2 6.0 %pack_first.1 = (bf16[14,128,128]{2,1,0:T(8,128)(2,1)}, bf16[14,128,128]{2,1,0:T(8,128)(2,1)}, bf16[14,128,128]{2,1,0:T(8,128)(2,1)}, bf16[96,128,128]{2,1,0:T(8,128)(2,1)}) custom-call(s32[8,128]{1,0:T(8,128)} %copy-done.2, bf16[32,128,128]{2,1,0:T(8,128)(2,1)S(1)} %bitcast.111, bf16[32,128,128]{2,1,0:T(8,128)(2,1)} %collective-permute-done.2.refs_1_.refs_4_, ...), custom_call_target="tpu_custom_call" | custom-call | tf_op jit(solution)/shard_map/pack_first/pallas_call | solution.py:281
  34.2 4.8 %all-to-all-start.3 = ((bf16[96,128,128]{2,1,0:T(8,128)(2,1)}), bf16[96,128,128]{2,1,0:T(8,128)(2,1)S(1)}, u32[]{:S(2)}, u32[]{:S(2)}) async-start(bf16[96,128,128]{2,1,0:T(8,128)(2,1)} %get-tuple-element.232), calls=%async_computation.8 | async-start | bytes 6291456 | tf_op jit(solution)/shard_map/all_to_all | solution.py:545
  39.0 0.3 collective-permute-start.4
  39.3 3.1 %collective-permute-start.5 = (bf16[14,128,128]{2,1,0:T(8,128)(2,1)}, bf16[14,128,128]{2,1,0:T(8,128)(2,1)S(1)}, u32[]{:S(2)}, u32[]{:S(2)}) collective-permute-start(bf16[14,128,128]{2,1,0:T(8,128)(2,1)} %get-tuple-element.235), channel_id=1, source_target_pairs={{0,16},{8,24},{16,0},{24,8},{1,17},{9,25},{17,1},{25,9},{2,18},{10... | collective-permute-start | bytes 1376264 | tf_op jit(solution)/shard_map/ppermute | solution.py:577
  42.4 7.8 %collective-permute-done.4.refs_1_ = bf16[14,128,128]{2,1,0:T(8,128)(2,1)S(1)} collective-permute-done((bf16[14,128,128]{2,1,0:T(8,128)(2,1)}, bf16[14,128,128]{2,1,0:T(8,128)(2,1)S(1)}, u32[]{:S(2)}, u32[]{:S(2)}) %collective-permute-start.4) | collective-permute-done | bytes 458784 | tf_op jit(solution)/shard_map/ppermute | solution.py:577
  50.2 21.3 %collective-permute-start.7 = (bf16[14,128,128]{2,1,0:T(8,128)(2,1)S(1)}, bf16[14,128,128]{2,1,0:T(8,128)(2,1)S(1)}, u32[]{:S(2)}, u32[]{:S(2)}) collective-permute-start(bf16[14,128,128]{2,1,0:T(8,128)(2,1)S(1)} %collective-permute-done.4.refs_1_), channel_id=1, source_target_pairs={{0,1},{1,0},{2,3},{3,2},{4,5},{5,4},{6,7},{7,6},{8,9},{9,8},{10,11... | collective-permute-start | bytes 1376264 | tf_op jit(solution)/shard_map/ppermute | solution.py:542
  71.4 6.4 %collective-permute-done.5.refs_2_ = bf16[14,128,128]{2,1,0:T(8,128)(2,1)S(1)} collective-permute-done((bf16[14,128,128]{2,1,0:T(8,128)(2,1)}, bf16[14,128,128]{2,1,0:T(8,128)(2,1)S(1)}, u32[]{:S(2)}, u32[]{:S(2)}) %collective-permute-start.5) | collective-permute-done | bytes 458784 | tf_op jit(solution)/shard_map/ppermute | solution.py:577
  77.9 2.0 %collective-permute-start.8 = (bf16[14,128,128]{2,1,0:T(8,128)(2,1)S(1)}, bf16[14,128,128]{2,1,0:T(8,128)(2,1)S(1)}, u32[]{:S(2)}, u32[]{:S(2)}) collective-permute-start(bf16[14,128,128]{2,1,0:T(8,128)(2,1)S(1)} %collective-permute-done.5.refs_2_), channel_id=1, source_target_pairs={{0,1},{1,0},{2,3},{3,2},{4,5},{5,4},{6,7},{7,6},{8,9},{9,8},{10,11... | collective-permute-start | bytes 1376264 | tf_op jit(solution)/shard_map/ppermute | solution.py:542
  79.8 1.7 %collective-permute-done.6.refs_3_ = bf16[14,128,128]{2,1,0:T(8,128)(2,1)S(1)} collective-permute-done((bf16[14,128,128]{2,1,0:T(8,128)(2,1)}, bf16[14,128,128]{2,1,0:T(8,128)(2,1)S(1)}, u32[]{:S(2)}, u32[]{:S(2)}) %collective-permute-start.6) | collective-permute-done | bytes 458784 | tf_op jit(solution)/shard_map/ppermute | solution.py:577
  81.6 1.3 collective-permute-start.9
  82.9 0.8 copy-done.24
  83.6 0.8 copy-done.25
  84.4 5.8 %pack_items.1 = (bf16[20,128,128]{2,1,0:T(8,128)(2,1)}, bf16[20,128,128]{2,1,0:T(8,128)(2,1)}, bf16[20,128,128]{2,1,0:T(8,128)(2,1)}, bf16[20,128,128]{2,1,0:T(8,128)(2,1)}) custom-call(s32[8,128]{1,0:T(8,128)} %copy-done.2, bf16[32,128,128]{2,1,0:T(8,128)(2,1)} %bitcast.109, bf16[14,128,128]{2,1,0:T(8,128)(2,1)} %copy-done.21, ...), custom_call_target="tpu_custom_call" | custom-call | tf_op jit(solution)/shard_map/pack_items/pallas_call | solution.py:281
  90.3 0.4 collective-permute-start.14
  90.7 1.2 collective-permute-start.10
  91.9 1.2 collective-permute-start.16
  93.1 0.3 collective-permute-start.18
  93.4 1.0 collective-permute-start.11
  94.4 1.9 %collective-permute-done.11 = f32[128,128]{1,0:T(8,128)S(1)} collective-permute-done((f32[128,128]{1,0:T(8,128)}, f32[128,128]{1,0:T(8,128)S(1)}, u32[]{:S(2)}, u32[]{:S(2)}) %collective-permute-start.11) | collective-permute-done | bytes 65568 | tf_op jit(solution)/shard_map/ppermute | solution.py:296
  96.3 0.8 add.203
  97.2 3.4 %collective-permute-done.12 = f32[128,128]{1,0:T(8,128)S(1)} collective-permute-done((f32[128,128]{1,0:T(8,128)S(1)}, f32[128,128]{1,0:T(8,128)S(1)}, u32[]{:S(2)}, u32[]{:S(2)}) %collective-permute-start.12) | collective-permute-done | bytes 65568 | tf_op jit(solution)/shard_map/ppermute | solution.py:296
  100.6 0.7 collective-permute-start.13
  101.4 3.7 %collective-permute-done.13 = f32[128,128]{1,0:T(8,128)S(1)} collective-permute-done((f32[128,128]{1,0:T(8,128)S(1)}, f32[128,128]{1,0:T(8,128)S(1)}, u32[]{:S(2)}, u32[]{:S(2)}) %collective-permute-start.13) | collective-permute-done | bytes 65568 | tf_op jit(solution)/shard_map/ppermute | solution.py:296
  105.0 2.1 %collective-permute-start.15 = (bf16[20,128,128]{2,1,0:T(8,128)(2,1)}, bf16[20,128,128]{2,1,0:T(8,128)(2,1)S(1)}, u32[]{:S(2)}, u32[]{:S(2)}) collective-permute-start(bf16[20,128,128]{2,1,0:T(8,128)(2,1)} %get-tuple-element.245.refs_2_), channel_id=1, source_target_pairs={{0,1},{1,0},{2,3},{3,2},{4,5},{5,4},{6,7},{7,6},{8,9},{9,8},{10,11... | collective-permute-start | bytes 1966088 | tf_op jit(solution)/shard_map/ppermute | solution.py:542
  107.1 1.0 collective-permute-done.10.refs_8_
  108.1 1.5 %collective-permute-start.20 = (bf16[20,128,128]{2,1,0:T(8,128)(2,1)S(1)}, bf16[20,128,128]{2,1,0:T(8,128)(2,1)S(1)}, u32[]{:S(2)}, u32[]{:S(2)}) collective-permute-start(bf16[20,128,128]{2,1,0:T(8,128)(2,1)S(1)} %collective-permute-done.10.refs_8_), channel_id=1, source_target_pairs={{0,1},{1,0},{2,3},{3,2},{4,5},{5,4},{6,7},{7,6},{8,9},{9,8},{10,11... | collective-permute-start | bytes 1966088 | tf_op jit(solution)/shard_map/ppermute | solution.py:542
  109.6 12.5 %collective-permute-done.16.refs_4_ = bf16[20,128,128]{2,1,0:T(8,128)(2,1)S(1)} collective-permute-done((bf16[20,128,128]{2,1,0:T(8,128)(2,1)}, bf16[20,128,128]{2,1,0:T(8,128)(2,1)S(1)}, u32[]{:S(2)}, u32[]{:S(2)}) %collective-permute-start.16) | collective-permute-done | bytes 655392 | tf_op jit(solution)/shard_map/ppermute | solution.py:595
  122.1 1.0 collective-permute-start.17
  123.1 0.6 slice.3
  124.3 0.5 collective-permute-done.17.refs_5_
  124.8 0.9 collective-permute-done.19.refs_7_
  125.7 1.1 copy-done.1
  126.8 15.6 %sweep.1 = f32[512,128]{1,0:T(8,128)} custom-call(s32[8,128]{1,0:T(8,128)S(1)} %copy-done.3, f32[512,128]{1,0:T(8,128)S(1)} %copy-done.15, f32[128,128]{1,0:T(8,128)S(1)} %add.205.gram_ref, bf16[96,128,128]{2,1,0:T(8,128)(2,1)S(1)} %all-to-all-done.3.refs_0_, bf16[96,128,128]{2,1,0:T(8,128)(2,1)S(1)} %collective-permute-done.14.refs_1_, ...), custom_call_target="tpu_custom_call" | custom-call | tf_op jit(solution)/shard_map/sweep/pallas_call | solution.py:241
  (44 shorter events, 0.3 us)
Async XLA Ops:
  6.5 4.1 %copy-start.5 = (bf16[4096,128]{1,0:T(8,128)(2,1)S(1)}, bf16[4096,128]{1,0:T(8,128)(2,1)}, u32[]{:S(2)}) copy-start(bf16[4096,128]{1,0:T(8,128)(2,1)} %param.18) | copy-start | bytes 3145732
  9.8 18.4 %copy-start = (bf16[64,128,128]{2,1,0:T(8,128)(2,1)}, bf16[64,128,128]{2,1,0:T(8,128)(2,1)S(1)}, u32[]{:S(2)}) copy-start(bf16[64,128,128]{2,1,0:T(8,128)(2,1)S(1)} %get-tuple-element.231.refs_2_) | copy-start | bytes 6291460
  9.8 1.8 %copy-start.26 = (s32[64]{0:T(128)S(1)}, s32[64]{0:T(128)}, u32[]{:S(2)}) copy-start(s32[64]{0:T(128)} %param.19) | copy-start | bytes 772
  9.9 1.8 %copy-start.27 = (s32[64]{0:T(128)S(1)}, s32[64]{0:T(128)}, u32[]{:S(2)}) copy-start(s32[64]{0:T(128)} %param.20) | copy-start | bytes 772
  9.9 18.3 %collective-permute-start.3 = (bf16[64,128,128]{2,1,0:T(8,128)(2,1)S(1)}, bf16[64,128,128]{2,1,0:T(8,128)(2,1)}, u32[]{:S(2)}, u32[]{:S(2)}) collective-permute-start(bf16[64,128,128]{2,1,0:T(8,128)(2,1)S(1)} %get-tuple-element.231.refs_2_), channel_id=1, source_target_pairs={{0,1},{1,0},{2,3},{3,2},{4,5},{5,4},{6,7},{7,6},{8,9},{9,8},{10,11... | collective-permute-start | bytes 6291464 | tf_op jit(solution)/shard_map/ppermute | solution.py:542
  10.6 17.6 %collective-permute-start.2 = (bf16[32,128,128]{2,1,0:T(8,128)(2,1)S(1)}, bf16[32,128,128]{2,1,0:T(8,128)(2,1)}, u32[]{:S(2)}, u32[]{:S(2)}) collective-permute-start(bf16[32,128,128]{2,1,0:T(8,128)(2,1)S(1)} %bitcast.110), channel_id=1, source_target_pairs={{0,1},{1,0},{2,3},{3,2},{4,5},{5,4},{6,7},{7,6},{8,9},{9,8},{10,11... | collective-permute-start | bytes 3145736 | tf_op jit(solution)/shard_map/ppermute | solution.py:542
  11.2 7.5 %collective-permute-start = (f32[128,128]{1,0:T(8,128)S(1)}, f32[128,128]{1,0:T(8,128)S(1)}, u32[]{:S(2)}, u32[]{:S(2)}) collective-permute-start(f32[128,128]{1,0:T(8,128)S(1)} %fusion.131), channel_id=1, source_target_pairs={{0,2},{1,3},{2,0},{3,1},{4,6},{5,7},{6,4},{7,5},{8,10},{9,11},{10,... | collective-permute-start | bytes 196616 | tf_op jit(solution)/shard_map/ppermute | solution.py:296
  12.3 11.1 %all-to-all-start.2 = ((s32[32,1,64]{2,1,0:T(1,128)}), s32[32,1,64]{2,1,0:T(1,128)S(1)}, u32[]{:S(2)}, u32[]{:S(2)}) async-start(s32[32,1,64]{2,1,0:T(1,128)} %broadcast_in_dim.41), calls=%async_computation.7 | async-start | bytes 32768 | tf_op jit(solution)/shard_map/all_to_all | solution.py:559
  18.7 8.9 %collective-permute-start.1 = (f32[128,128]{1,0:T(8,128)S(1)}, f32[128,128]{1,0:T(8,128)S(1)}, u32[]{:S(2)}, u32[]{:S(2)}) collective-permute-start(f32[128,128]{1,0:T(8,128)S(1)} %add.201), channel_id=1, source_target_pairs={{0,4},{1,5},{2,6},{3,7},{4,0},{5,1},{6,2},{7,3},{8,12},{9,13},{10,... | collective-permute-start | bytes 196616 | tf_op jit(solution)/shard_map/ppermute | solution.py:296
  27.0 0.6 copy-start.2
  34.2 56.0 %all-to-all-start.3 = ((bf16[96,128,128]{2,1,0:T(8,128)(2,1)}), bf16[96,128,128]{2,1,0:T(8,128)(2,1)S(1)}, u32[]{:S(2)}, u32[]{:S(2)}) async-start(bf16[96,128,128]{2,1,0:T(8,128)(2,1)} %get-tuple-element.232), calls=%async_computation.8 | async-start | bytes 6291456 | tf_op jit(solution)/shard_map/all_to_all | solution.py:545
  39.0 11.2 %collective-permute-start.4 = (bf16[14,128,128]{2,1,0:T(8,128)(2,1)}, bf16[14,128,128]{2,1,0:T(8,128)(2,1)S(1)}, u32[]{:S(2)}, u32[]{:S(2)}) collective-permute-start(bf16[14,128,128]{2,1,0:T(8,128)(2,1)} %get-tuple-element.234), channel_id=1, source_target_pairs={{0,8},{8,16},{16,24},{24,0},{1,9},{9,17},{17,25},{25,1},{2,10},{10... | collective-permute-start | bytes 1376264 | tf_op jit(solution)/shard_map/ppermute | solution.py:577
  39.3 38.6 %collective-permute-start.5 = (bf16[14,128,128]{2,1,0:T(8,128)(2,1)}, bf16[14,128,128]{2,1,0:T(8,128)(2,1)S(1)}, u32[]{:S(2)}, u32[]{:S(2)}) collective-permute-start(bf16[14,128,128]{2,1,0:T(8,128)(2,1)} %get-tuple-element.235), channel_id=1, source_target_pairs={{0,16},{8,24},{16,0},{24,8},{1,17},{9,25},{17,1},{25,9},{2,18},{10... | collective-permute-start | bytes 1376264 | tf_op jit(solution)/shard_map/ppermute | solution.py:577
  42.4 80.7 %copy-start.3 = (s32[8,128]{1,0:T(8,128)S(1)}, s32[8,128]{1,0:T(8,128)}, u32[]{:S(2)}) copy-start(s32[8,128]{1,0:T(8,128)} %copy-done.2) | copy-start | bytes 12292
  42.4 83.4 %copy-start.15 = (f32[512,128]{1,0:T(8,128)S(1)}, f32[512,128]{1,0:T(8,128)}, u32[]{:S(2)}) copy-start(f32[512,128]{1,0:T(8,128)} %prior_ref.1) | copy-start | bytes 786436
  42.4 39.2 %collective-permute-start.6 = (bf16[14,128,128]{2,1,0:T(8,128)(2,1)}, bf16[14,128,128]{2,1,0:T(8,128)(2,1)S(1)}, u32[]{:S(2)}, u32[]{:S(2)}) collective-permute-start(bf16[14,128,128]{2,1,0:T(8,128)(2,1)} %get-tuple-element.236), channel_id=1, source_target_pairs={{0,24},{8,0},{16,8},{24,16},{1,25},{9,1},{17,9},{25,17},{2,26},{10... | collective-permute-start | bytes 1376264 | tf_op jit(solution)/shard_map/ppermute | solution.py:577
  50.2 34.3 %copy-start.21 = (bf16[14,128,128]{2,1,0:T(8,128)(2,1)}, bf16[14,128,128]{2,1,0:T(8,128)(2,1)S(1)}, u32[]{:S(2)}) copy-start(bf16[14,128,128]{2,1,0:T(8,128)(2,1)S(1)} %collective-permute-done.4.refs_1_) | copy-start | bytes 1376260
  50.2 32.7 %collective-permute-start.7 = (bf16[14,128,128]{2,1,0:T(8,128)(2,1)S(1)}, bf16[14,128,128]{2,1,0:T(8,128)(2,1)S(1)}, u32[]{:S(2)}, u32[]{:S(2)}) collective-permute-start(bf16[14,128,128]{2,1,0:T(8,128)(2,1)S(1)} %collective-permute-done.4.refs_1_), channel_id=1, source_target_pairs={{0,1},{1,0},{2,3},{3,2},{4,5},{5,4},{6,7},{7,6},{8,9},{9,8},{10,11... | collective-permute-start | bytes 1376264 | tf_op jit(solution)/shard_map/ppermute | solution.py:542
  77.9 5.0 %copy-start.22 = (bf16[14,128,128]{2,1,0:T(8,128)(2,1)}, bf16[14,128,128]{2,1,0:T(8,128)(2,1)S(1)}, u32[]{:S(2)}) copy-start(bf16[14,128,128]{2,1,0:T(8,128)(2,1)S(1)} %collective-permute-done.5.refs_2_) | copy-start | bytes 1376260
  77.9 5.0 %collective-permute-start.8 = (bf16[14,128,128]{2,1,0:T(8,128)(2,1)S(1)}, bf16[14,128,128]{2,1,0:T(8,128)(2,1)S(1)}, u32[]{:S(2)}, u32[]{:S(2)}) collective-permute-start(bf16[14,128,128]{2,1,0:T(8,128)(2,1)S(1)} %collective-permute-done.5.refs_2_), channel_id=1, source_target_pairs={{0,1},{1,0},{2,3},{3,2},{4,5},{5,4},{6,7},{7,6},{8,9},{9,8},{10,11... | collective-permute-start | bytes 1376264 | tf_op jit(solution)/shard_map/ppermute | solution.py:542
  81.6 1.3 copy-start.23
  81.6 2.9 %collective-permute-start.9 = (bf16[14,128,128]{2,1,0:T(8,128)(2,1)S(1)}, bf16[14,128,128]{2,1,0:T(8,128)(2,1)}, u32[]{:S(2)}, u32[]{:S(2)}) collective-permute-start(bf16[14,128,128]{2,1,0:T(8,128)(2,1)S(1)} %collective-permute-done.6.refs_3_), channel_id=1, source_target_pairs={{0,1},{1,0},{2,3},{3,2},{4,5},{5,4},{6,7},{7,6},{8,9},{9,8},{10,11... | collective-permute-start | bytes 1376264 | tf_op jit(solution)/shard_map/ppermute | solution.py:542
  82.9 0.8 copy-start.24
  83.6 0.8 copy-start.25
  90.3 35.5 %collective-permute-start.14 = (bf16[96,128,128]{2,1,0:T(8,128)(2,1)S(1)}, bf16[96,128,128]{2,1,0:T(8,128)(2,1)S(1)}, u32[]{:S(2)}, u32[]{:S(2)}) collective-permute-start(bf16[96,128,128]{2,1,0:T(8,128)(2,1)S(1)} %all-to-all-done.3.refs_0_), channel_id=1, source_target_pairs={{0,1},{1,0},{2,3},{3,2},{4,5},{5,4},{6,7},{7,6},{8,9},{9,8},{10,11... | collective-permute-start | bytes 9437192 | tf_op jit(solution)/shard_map/ppermute | solution.py:542
  90.7 17.3 %collective-permute-start.10 = (bf16[20,128,128]{2,1,0:T(8,128)(2,1)}, bf16[20,128,128]{2,1,0:T(8,128)(2,1)S(1)}, u32[]{:S(2)}, u32[]{:S(2)}) collective-permute-start(bf16[20,128,128]{2,1,0:T(8,128)(2,1)} %get-tuple-element.241), channel_id=1, source_target_pairs={{0,6},{1,7},{2,4},{3,5},{4,2},{5,3},{6,0},{7,1},{8,14},{9,15},{10,... | collective-permute-start | bytes 1966088 | tf_op jit(solution)/shard_map/ppermute | solution.py:595
  91.9 30.2 %collective-permute-start.16 = (bf16[20,128,128]{2,1,0:T(8,128)(2,1)}, bf16[20,128,128]{2,1,0:T(8,128)(2,1)S(1)}, u32[]{:S(2)}, u32[]{:S(2)}) collective-permute-start(bf16[20,128,128]{2,1,0:T(8,128)(2,1)} %get-tuple-element.246), channel_id=1, source_target_pairs={{0,2},{1,3},{2,0},{3,1},{4,6},{5,7},{6,4},{7,5},{8,10},{9,11},{10,... | collective-permute-start | bytes 1966088 | tf_op jit(solution)/shard_map/ppermute | solution.py:595
  93.1 30.0 %collective-permute-start.18 = (bf16[20,128,128]{2,1,0:T(8,128)(2,1)}, bf16[20,128,128]{2,1,0:T(8,128)(2,1)S(1)}, u32[]{:S(2)}, u32[]{:S(2)}) collective-permute-start(bf16[20,128,128]{2,1,0:T(8,128)(2,1)} %get-tuple-element.247), channel_id=1, source_target_pairs={{0,4},{1,5},{2,6},{3,7},{4,0},{5,1},{6,2},{7,3},{8,12},{9,13},{10,... | collective-permute-start | bytes 1966088 | tf_op jit(solution)/shard_map/ppermute | solution.py:595
  93.4 2.9 %collective-permute-start.11 = (f32[128,128]{1,0:T(8,128)}, f32[128,128]{1,0:T(8,128)S(1)}, u32[]{:S(2)}, u32[]{:S(2)}) collective-permute-start(f32[128,128]{1,0:T(8,128)} %add.202), channel_id=1, source_target_pairs={{0,1},{1,0},{2,3},{3,2},{4,5},{5,4},{6,7},{7,6},{8,9},{9,8},{10,11... | collective-permute-start | bytes 196616 | tf_op jit(solution)/shard_map/ppermute | solution.py:296
  97.2 3.5 %collective-permute-start.12 = (f32[128,128]{1,0:T(8,128)S(1)}, f32[128,128]{1,0:T(8,128)S(1)}, u32[]{:S(2)}, u32[]{:S(2)}) collective-permute-start(f32[128,128]{1,0:T(8,128)S(1)} %add.203), channel_id=1, source_target_pairs={{0,8},{8,0},{16,24},{24,16},{1,9},{9,1},{17,25},{25,17},{2,10},{10... | collective-permute-start | bytes 196616 | tf_op jit(solution)/shard_map/ppermute | solution.py:296
  100.6 4.4 %collective-permute-start.13 = (f32[128,128]{1,0:T(8,128)S(1)}, f32[128,128]{1,0:T(8,128)S(1)}, u32[]{:S(2)}, u32[]{:S(2)}) collective-permute-start(f32[128,128]{1,0:T(8,128)S(1)} %add.204), channel_id=1, source_target_pairs={{0,16},{8,24},{16,0},{24,8},{1,17},{9,25},{17,1},{25,9},{2,18},{10... | collective-permute-start | bytes 196616 | tf_op jit(solution)/shard_map/ppermute | solution.py:296
  105.0 19.3 %collective-permute-start.15 = (bf16[20,128,128]{2,1,0:T(8,128)(2,1)}, bf16[20,128,128]{2,1,0:T(8,128)(2,1)S(1)}, u32[]{:S(2)}, u32[]{:S(2)}) collective-permute-start(bf16[20,128,128]{2,1,0:T(8,128)(2,1)} %get-tuple-element.245.refs_2_), channel_id=1, source_target_pairs={{0,1},{1,0},{2,3},{3,2},{4,5},{5,4},{6,7},{7,6},{8,9},{9,8},{10,11... | collective-permute-start | bytes 1966088 | tf_op jit(solution)/shard_map/ppermute | solution.py:542
  108.1 16.3 %collective-permute-start.20 = (bf16[20,128,128]{2,1,0:T(8,128)(2,1)S(1)}, bf16[20,128,128]{2,1,0:T(8,128)(2,1)S(1)}, u32[]{:S(2)}, u32[]{:S(2)}) collective-permute-start(bf16[20,128,128]{2,1,0:T(8,128)(2,1)S(1)} %collective-permute-done.10.refs_8_), channel_id=1, source_target_pairs={{0,1},{1,0},{2,3},{3,2},{4,5},{5,4},{6,7},{7,6},{8,9},{9,8},{10,11... | collective-permute-start | bytes 1966088 | tf_op jit(solution)/shard_map/ppermute | solution.py:542
  122.1 2.7 %collective-permute-start.17 = (bf16[20,128,128]{2,1,0:T(8,128)(2,1)S(1)}, bf16[20,128,128]{2,1,0:T(8,128)(2,1)S(1)}, u32[]{:S(2)}, u32[]{:S(2)}) collective-permute-start(bf16[20,128,128]{2,1,0:T(8,128)(2,1)S(1)} %collective-permute-done.16.refs_4_), channel_id=1, source_target_pairs={{0,1},{1,0},{2,3},{3,2},{4,5},{5,4},{6,7},{7,6},{8,9},{9,8},{10,11... | collective-permute-start | bytes 1966088 | tf_op jit(solution)/shard_map/ppermute | solution.py:542
  123.1 2.7 %collective-permute-start.19 = (bf16[20,128,128]{2,1,0:T(8,128)(2,1)S(1)}, bf16[20,128,128]{2,1,0:T(8,128)(2,1)S(1)}, u32[]{:S(2)}, u32[]{:S(2)}) collective-permute-start(bf16[20,128,128]{2,1,0:T(8,128)(2,1)S(1)} %collective-permute-done.18.refs_6_), channel_id=1, source_target_pairs={{0,1},{1,0},{2,3},{3,2},{4,5},{5,4},{6,7},{7,6},{8,9},{9,8},{10,11... | collective-permute-start | bytes 1966088 | tf_op jit(solution)/shard_map/ppermute | solution.py:542
  125.7 1.1 copy-start.1
where the time goes:
time: 152 us; the launch traced here: 149 us
  starting transfers between devices  50.9 us (33%)
  waiting for transfers between devices  43.2 us (28%)
  Pallas kernels  33.1 us (22%)
  between operations  14.2 us (9%)
  local copies, waits for them, and re-layouts  5.06 us (3%)
  other arithmetic  2.39 us (2%)
    ppermute x10, starting transfers between devices, swap(): return lax.ppermute(value, 'grp', [(i, i ^ 1) for i in range(n_grp)])  30.4 us
    ppermute x3, waiting for transfers between devices, body(): lax.ppermute(piece, 'blk', [(i, (i + 1 + shift) % n_blk) for i in range(n...  15.9 us
    pallas_call x1, Pallas kernels, run_sweep(): pl.pallas_call(functools.partial(sweep_kernel, len(count_pieces)), out_sh...  15.6 us
    ppermute x3, waiting for transfers between devices, body(): piece = lax.ppermute(piece, 'grp', [(i, i ^ 2 * off) for i in range(n_grp)])  13.5 us
    pallas_call x2, Pallas kernels, pack_tiles(): pl.pallas_call(functools.partial(pack_kernel, len(sources), len(lengths),...  11.8 us
    ppermute x5, waiting for transfers between devices, sum_with(): lax.ppermute(value, axis, [(i, i ^ bit) for i in range(size)])  9.02 us
    all_to_all x1, starting transfers between devices, body(): lax.all_to_all(jnp.broadcast_to(packed, (n_all, pairs)), ('blk', 'grp'),...  6.39 us
    all_to_all x1, starting transfers between devices, to_chips(): lax.all_to_all(value, 'grp', split_axis=0, concat_axis=0, tiled=True, axi...  4.76 us
  transfers between devices with their start and end apart: 23, of which 11 were waited for; matrix products, arithmetic and copies ran while one was open for 3% of the time, Pallas kernels for 5%

commit v1 on v0

--- a/solution.py
+++ b/solution.py
@@ -15,7 +15,9 @@
 
 FAR_CAP = 14
 COUNT_CAP = 24
-ITEM_CAP = 20
+NEAR_CAP = 8
+ITEM_CAP = 16
+RIDE = COUNT_CAP + NEAR_CAP
 LOADS = 128
 SPAN = 2
 VMEM_GRANT = 60 * 2**20
@@ -144,11 +146,14 @@
     among(0, len(sources))
 
 
-def sweep_kernel(n_counts, plan, prior_ref, gram_ref, *refs):
+def sweep_kernel(plan, prior_ref, gram_ref, *refs):
     weights, factors, low, image, residual, direction = refs[-6:]
-    count_pieces, item_pieces, out_ref = refs[:n_counts], refs[n_counts:-7], refs[-7]
+    item_pieces, out_ref = refs[:-7], refs[-7]
+    count_pieces = item_pieces[:2]
     tile, rank = factors.shape[1:]
-    rounds = plan[6, 0]
+    n_chunks = plan[6, 0]
+    halves = (n_chunks + TOGETHER // 2 - 1) // (TOGETHER // 2)
+    rounds = halves // 2
 
     def bring(place, carry):
         count_at = plan[3, place]
@@ -166,17 +171,17 @@
 
         return carry
 
-    lax.fori_loop(0, rounds * (TOGETHER * SPAN), bring, 0)
+    lax.fori_loop(0, halves * (TOGETHER // 2 * SPAN), bring, 0)
 
     def pair_images(with_rhs):
         image[...] = jnp.zeros_like(image)
         if with_rhs:
             residual[...] = jnp.zeros_like(residual)
 
-        def one_round(step, carry):
+        def some(first, n):
             shares = []
-            for number in range(TOGETHER):
-                chunk = step * TOGETHER + number
+            for number in range(n):
+                chunk = first + number
                 rows = pl.ds(pl.multiple_of(plan[5, chunk] * tile, tile), tile)
                 items = factors[pl.ds(chunk * SPAN, SPAN)].reshape(SPAN * tile, rank)
                 scaled = jnp.concatenate(
@@ -200,9 +205,13 @@
                 image[rows, :] += back
                 if with_rhs:
                     residual[rows, :] += pulled
+
+        def one_round(step, carry):
+            some(step * TOGETHER, TOGETHER)
             return carry
 
         lax.fori_loop(0, rounds, one_round, 0)
+        pl.when(halves % 2 == 1)(lambda: some(rounds * TOGETHER, TOGETHER // 2))
 
     def gram_term(vectors):
         return jnp.dot(
@@ -233,13 +242,12 @@
             norm_now = fresh
 
 
-def run_sweep(plan, user_prior, gram, count_pieces, item_pieces):
+def run_sweep(plan, user_prior, gram, pieces):
     own_rows, rank = user_prior.shape
-    tile = count_pieces[0].shape[1]
-    pieces = [*count_pieces, *item_pieces]
+    tile = pieces[0].shape[1]
     vmem = pl.BlockSpec(memory_space=pltpu.VMEM)
     return pl.pallas_call(
-        functools.partial(sweep_kernel, len(count_pieces)),
+        sweep_kernel,
         out_shape=jax.ShapeDtypeStruct((own_rows, rank), jnp.float32),
         in_specs=[pl.BlockSpec(memory_space=pltpu.SMEM)] + [vmem] * (2 + len(pieces)),
         out_specs=vmem,
@@ -367,8 +375,14 @@
         excess = jnp.maximum(excess, worst(asks, 2 * FAR_CAP))
         to_chip = lax.shift_right_logical(user, bits_for(own_tiles) + 1)
         to = one_hot(to_chip, n_chips).astype(jnp.float32)
-        for key, cap in ((from_chip, COUNT_CAP), (chip & (n_chips - 1), ITEM_CAP)):
-            loads = dot_nt((one_hot(key, n_chips) & live).astype(jnp.float32), to)
+        column = chip & (n_chips - 1)
+        near = lax.shift_right_logical(chip, bits_for(n_chips)) == blk
+        for key, inside, cap in (
+            (from_chip, live, COUNT_CAP),
+            (column, live & near, NEAR_CAP),
+            (column, live & ~near, ITEM_CAP),
+        ):
+            loads = dot_nt((one_hot(key, n_chips) & inside).astype(jnp.float32), to)
             excess = jnp.maximum(excess, worst(loads, 2 * cap))
         loads = jnp.sum(
             (one_hot(user, user_blocks) & live).astype(jnp.int32), axis=1, keepdims=True
@@ -407,12 +421,17 @@
     to_chip = lax.shift_right_logical(owner, 1)
     column = chip & (n_chips - 1)
     to_me = live & (owner == my_grp)
+    shift = (my_blk + n_blk - lax.shift_right_logical(chip, bits_for(n_chips))) & (n_blk - 1)
+    near, far = live & (shift == 0), live & (shift > 0)
+    in_tile = one_hot(local_user, own_tiles) & to_me
     groups = [
         one_hot(to_chip, n_chips) & (live & (from_chip == my_chip)),
         one_hot(from_chip, n_chips) & (live & (to_chip == my_chip)),
-        one_hot(to_chip, n_chips) & (live & (column == my_chip)),
-        one_hot(column, n_chips) & (live & (to_chip == my_chip)),
-        one_hot(local_user, own_tiles) & to_me,
+        one_hot(to_chip, n_chips) & (near & (column == my_chip)),
+        one_hot(column, n_chips) & (near & (to_chip == my_chip)),
+        one_hot(to_chip, n_chips) & (far & (column == my_chip)),
+        one_hot(column, n_chips) & (far & (to_chip == my_chip)),
+        in_tile,
     ]
     before = (iota(n_entries, n_entries, 0) < iota(n_entries, n_entries, 1)).astype(jnp.float32)
     before = before.astype(jnp.bfloat16)
@@ -424,26 +443,32 @@
         )
         earlier = jnp.sum(jnp.where(marks, earlier, 0.0), axis=0, keepdims=True)
         ranks.append(earlier.astype(jnp.int32))
-    counts_out, counts_back, items_out, items_back, user_rank = ranks
+    counts_out, counts_back, near_out, near_back, far_out, far_back, user_rank = ranks
 
     half = lambda rank: lax.shift_right_logical(rank, 1)
     sent = lambda rank, cap: live & ((rank & 1) == my_core) & (half(rank) < cap)
+    back = lambda rank, cap: jnp.minimum(half(rank), cap - 1)
+    core = lambda rank: (rank & 1) ^ my_core
     (out_ref[0:1, :],) = choose(
         to_chip * COUNT_CAP + half(counts_out), sent(counts_out, COUNT_CAP) & (from_chip == my_chip),
         width, at_source((source & 1) ^ my_core, index & (pairs - 1), 2),
     )
     out_ref[1:2, :] = asked
-    shift = (my_blk + n_blk - lax.shift_right_logical(chip, bits_for(n_chips))) & (n_blk - 1)
-    near = shift == 0
-    lane = jnp.where(near, lax.shift_right_logical(held, bits_for(tiles_held)), far_place & 1)
-    row = jnp.where(near, held & (tiles_held - 1), half(far_place))
+    (out_ref[7:8, :],) = choose(
+        to_chip * NEAR_CAP + half(near_out), near & (column == my_chip) & sent(near_out, NEAR_CAP),
+        width,
+        at_source(
+            lax.shift_right_logical(held, bits_for(tiles_held)) ^ my_core, held & (tiles_held - 1), 2
+        ),
+    )
     (out_ref[2:3, :],) = choose(
-        (to_chip ^ my_chip) * ITEM_CAP + half(items_out),
-        sent(items_out, ITEM_CAP) & (column == my_chip),
-        width, at_source((lane ^ my_core) * n_blk + shift, row, 2 * n_blk),
-    )
-
-    in_tile = groups[4]
+        (to_chip ^ my_chip) * ITEM_CAP + half(far_out),
+        far & (column == my_chip) & sent(far_out, ITEM_CAP), width,
+        at_source(
+            core(far_place) * (n_blk - 1) + shift - 1, half(far_place), 2 * (n_blk - 1)
+        ),
+    )
+
     loads = jnp.sum(in_tile.astype(jnp.int32), axis=1, keepdims=True)
     chunks = lax.shift_right_logical(loads + SPAN - 1, bits_for(SPAN)).astype(jnp.float32)
     rows = chunks.shape[0]
@@ -456,11 +481,18 @@
     room_at = jnp.sum(jnp.where(in_tile, firsts * SPAN, 0.0), axis=0, keepdims=True)
     room_at = room_at.astype(jnp.int32) + user_rank
     hit = to_me & (room_at < LOADS)
-    counts_row = jnp.minimum(half(counts_back), COUNT_CAP - 1)
-    items_row = jnp.minimum(half(items_back), ITEM_CAP - 1)
-    count_at = at_source((counts_back & 1) ^ my_core, from_chip * COUNT_CAP + counts_row, 2)
-    item_at = at_source(
-        (column ^ my_chip) * 2 + ((items_back & 1) ^ my_core), items_row, 2 * n_chips
+    count_at = at_source(
+        core(counts_back), from_chip * RIDE + back(counts_back, COUNT_CAP), 2
+    )
+    n_sources = 2 + 2 * n_chips
+    item_at = jnp.where(
+        shift == 0,
+        at_source(
+            core(near_back), column * RIDE + COUNT_CAP + back(near_back, NEAR_CAP), n_sources
+        ),
+        at_source(
+            2 + (column ^ my_chip) * 2 + core(far_back), back(far_back, ITEM_CAP), n_sources
+        ),
     )
     out_ref[3:4, :], out_ref[4:5, :] = choose(room_at, hit, width, count_at + 1, item_at)
     passed = (iota(rows, width, 1).astype(jnp.float32) >= ends[:, :1]) & (
@@ -468,14 +500,12 @@
     )
     out_ref[5:6, :] = jnp.sum(passed.astype(jnp.int32), axis=0, keepdims=True)
     total = ends[own_tiles - 1:own_tiles, :1].astype(jnp.int32)
-    rounds = lax.shift_right_logical(total + TOGETHER - 1, bits_for(TOGETHER))
-    rounds = jnp.minimum(rounds, LOADS // (SPAN * TOGETHER))
+    total = jnp.minimum(total, LOADS // SPAN)
     copies = jnp.sum(hit.astype(jnp.int32), axis=1, keepdims=True)
     at = iota(1, width, 1)
     fits = (excess <= 0.0).astype(jnp.int32)
-    head = jnp.where(at == 0, rounds, jnp.where(at == 1, copies, jnp.where(at == 2, fits, 0)))
+    head = jnp.where(at == 0, total, jnp.where(at == 1, copies, jnp.where(at == 2, fits, 0)))
     out_ref[6:7, :] = head
-    out_ref[7:8, :] = jnp.zeros((1, width), jnp.int32)
 
 
 def route(every, my_blk, my_grp, n_grp, own_tiles, tiles_held):
@@ -557,8 +587,7 @@
     scaled_mate = swap(scaled)
     packed = (item_tiles * 2 + live.astype(jnp.int32)) * user_blocks + user_tiles
     every = lax.all_to_all(
-        jnp.broadcast_to(packed, (n_all, pairs)), ("blk", "grp"),
-        split_axis=0, concat_axis=0, tiled=True,
+        jnp.broadcast_to(packed, (n_all, pairs)), ("blk", "grp"), split_axis=0, concat_axis=0
     )
     table = route(every.reshape(n_blk, n_grp * pairs), my_blk, my_grp, n_grp, own_tiles, tiles_held)
     gram = gram_local
@@ -568,8 +597,10 @@
 
     jobs = [(0, 2, 1, shift * FAR_CAP, FAR_CAP, shift, 0) for shift in range(n_blk - 1)]
     for chip in range(n_chips):
-        jobs.append((2, 4, 0, chip * COUNT_CAP, COUNT_CAP, n_blk - 1, chip * COUNT_CAP))
-    lengths = [FAR_CAP] * (n_blk - 1) + [n_chips * COUNT_CAP]
+        ride = chip * RIDE
+        jobs.append((2, 4, 0, chip * COUNT_CAP, COUNT_CAP, n_blk - 1, ride))
+        jobs.append((0, 2, 7, chip * NEAR_CAP, NEAR_CAP, n_blk - 1, ride + COUNT_CAP))
+    lengths = [FAR_CAP] * (n_blk - 1) + [n_chips * RIDE]
     *far, counts_out = pack_tiles(
         "pack_first", table, [held, held_mate, scaled, scaled_mate], lengths, jobs
     )
@@ -580,23 +611,23 @@
     far_mate = [swap(piece) for piece in far]
     counts_own = to_chips(counts_out)
 
-    jobs = [(0, 2 * n_blk, 2, off * ITEM_CAP, ITEM_CAP, off, 0) for off in range(n_chips)]
+    jobs = [(0, 2 * (n_blk - 1), 2, off * ITEM_CAP, ITEM_CAP, off, 0) for off in range(n_chips)]
     items_out = pack_tiles(
-        "pack_items", table, [held, *far, held_mate, *far_mate], [ITEM_CAP] * n_chips, jobs
+        "pack_items", table, [*far, *far_mate], [ITEM_CAP] * n_chips, jobs
     )
     counts_own, gram, *items_out = lax.optimization_barrier((counts_own, gram, *items_out))
     counts_mate = swap(counts_own)
     gram = sum_with(gram, "grp", grp_bits[0])
     for bit in blk_bits:
         gram = sum_with(gram, "blk", bit)
-    item_pieces = []
+    item_pieces = [counts_own, counts_mate]
     for off, piece in enumerate(items_out):
         if off:
             piece = lax.ppermute(piece, "grp", [(i, i ^ (2 * off)) for i in range(n_grp)])
         if off == n_chips - 1:
             piece, gram = lax.optimization_barrier((piece, gram))
         item_pieces += [piece, swap(piece)]
-    by_owner = run_sweep(table, user_prior, gram, [counts_own, counts_mate], item_pieces)
+    by_owner = run_sweep(table, user_prior, gram, item_pieces)
 
     fits = table[6, 2] > 0
     return lax.cond(

time: 152 us -> 146 us (0.961); the launches traced: 149 us -> 146 us
  waiting for transfers between devices: 43.2 us -> 41.1 us
  local copies, waits for them, and re-layouts: 5.06 us -> 3.49 us
    ppermute x3, waiting for transfers between devices: 13.5 us -> 8.83 us  [body(): piece = lax.ppermute(piece, 'grp', [(i, i ^ 2 * off) for i in range(n_grp)])]
    ppermute x10, starting transfers between devices: 30.4 us -> 28.6 us  [swap(): return lax.ppermute(value, 'grp', [(i, i ^ 1) for i in range(n_grp)])]
    pallas_call x1, Pallas kernels: 15.6 us -> 17.3 us  [run_sweep(): pl.pallas_call(sweep_kernel, out_shape=jax.ShapeDtypeStruct((own_rows, ra...]
    unnamed x26 -> x32, local copies, waits for them, and re-layouts: 3.28 us -> 1.7 us
where the time goes in v1:
time: 146 us
  starting transfers between devices  50.5 us (35%)
  waiting for transfers between devices  41.1 us (28%)
  Pallas kernels  34.2 us (23%)
  between operations  14.3 us (10%)
  local copies, waits for them, and re-layouts  3.49 us (2%)
  other arithmetic  1.55 us (1%)
    ppermute x10, starting transfers between devices, swap(): return lax.ppermute(value, 'grp', [(i, i ^ 1) for i in range(n_grp)])  28.6 us
    pallas_call x1, Pallas kernels, run_sweep(): pl.pallas_call(sweep_kernel, out_shape=jax.ShapeDtypeStruct((own_rows, ra...  17.3 us
    ppermute x3, waiting for transfers between devices, body(): lax.ppermute(piece, 'blk', [(i, (i + 1 + shift) % n_blk) for i in range(n...  16 us
    pallas_call x2, Pallas kernels, pack_tiles(): pl.pallas_call(functools.partial(pack_kernel, len(sources), len(lengths),...  11 us
    ppermute x5, waiting for transfers between devices, sum_with(): lax.ppermute(value, axis, [(i, i ^ bit) for i in range(size)])  10.3 us
    ppermute x3, waiting for transfers between devices, body(): piece = lax.ppermute(piece, 'grp', [(i, i ^ 2 * off) for i in range(n_grp)])  8.83 us
    all_to_all x1, starting transfers between devices, body(): lax.all_to_all(jnp.broadcast_to(packed, (n_all, pairs)), ('blk', 'grp'),...  6.39 us
    all_to_all x1, starting transfers between devices, to_chips(): lax.all_to_all(value, 'grp', split_axis=0, concat_axis=0, tiled=True, axi...  6.07 us
  transfers between devices with their start and end apart: 23, of which 11 were waited for; matrix products, arithmetic and copies ran while one was open for 3% of the time, Pallas kernels for 5%

profile of v1, /device:TPU:11, one launch (start us, length us, event | category | flops | bytes accessed | tf_op | source)
XLA Modules:
  0.0 145.6 jit_solution(16281545355621680863)
XLA Ops:
  6.5 3.3 %scan_counts.1 = (bf16[64,128,128]{2,1,0:T(8,128)(2,1)S(1)}, s32[64,128]{1,0:T(8,128)S(1)}) custom-call(s32[64,128,128]{2,1,0:T(8,128)} %counts_ref.1), custom_call_target="tpu_custom_call" | custom-call | tf_op jit(solution)/shard_map/scan_counts/pallas_call | solution.py:536
  9.9 0.7 collective-permute-start.3
  10.6 0.1 collective-permute-start.2
  10.7 0.5 fusion.131
  11.2 0.3 collective-permute-start
  11.5 0.1 compare_reduce_fusion
  11.6 0.6 broadcast_in_dim.41
  12.3 6.4 %all-to-all-start.2 = ((s32[32,1,64]{2,1,0:T(1,128)}), s32[32,1,64]{2,1,0:T(1,128)S(1)}, u32[]{:S(2)}, u32[]{:S(2)}) async-start(s32[32,1,64]{2,1,0:T(1,128)} %broadcast_in_dim.41), calls=%async_computation.7 | async-start | bytes 32768 | tf_op jit(solution)/shard_map/all_to_all | solution.py:589
  18.7 1.2 collective-permute-start.1
  19.9 0.1 pad_add_fusion.spot
  20.0 3.3 %all-to-all-done.2 = s32[32,1,64]{2,1,0:T(1,128)S(1)} async-done(((s32[32,1,64]{2,1,0:T(1,128)}), s32[32,1,64]{2,1,0:T(1,128)S(1)}, u32[]{:S(2)}, u32[]{:S(2)}) %all-to-all-start.2) | async-done | bytes 8224 | tf_op jit(solution)/shard_map/all_to_all | solution.py:589
  23.3 0.5 broadcast.304
  23.8 0.7 reduce.3
  24.5 0.1 reshape.144.every_ref
  24.6 2.6 %route.1.table.plan = s32[8,128]{1,0:T(8,128)S(1)} custom-call(s32[2]{0:T(128)S(1)} %pad_add_fusion.spot, s32[4,512]{1,0:T(4,128)S(1)} %reshape.144.every_ref), custom_call_target="tpu_custom_call" | custom-call | tf_op jit(solution)/shard_map/route/pallas_call | solution.py:517
  27.2 0.6 copy-done.2
  27.8 0.6 add.202
  28.5 6.7 %pack_first.1 = (bf16[14,128,128]{2,1,0:T(8,128)(2,1)}, bf16[14,128,128]{2,1,0:T(8,128)(2,1)}, bf16[14,128,128]{2,1,0:T(8,128)(2,1)}, bf16[128,128,128]{2,1,0:T(8,128)(2,1)}) custom-call(s32[8,128]{1,0:T(8,128)} %copy-done.2, bf16[32,128,128]{2,1,0:T(8,128)(2,1)S(1)} %bitcast.110, bf16[32,128,128]{2,1,0:T(8,128)(2,1)} %collective-permute-done.2.refs_1_, ...), custom_call_target="tpu_custom_call" | custom-call | tf_op jit(solution)/shard_map/pack_first/pallas_call | solution.py:289
  35.2 6.1 %all-to-all-start.3 = ((bf16[128,128,128]{2,1,0:T(8,128)(2,1)}), bf16[128,128,128]{2,1,0:T(8,128)(2,1)}, u32[]{:S(2)}, u32[]{:S(2)}) async-start(bf16[128,128,128]{2,1,0:T(8,128)(2,1)} %get-tuple-element.232), calls=%async_computation.8 | async-start | bytes 8388608 | tf_op jit(solution)/shard_map/all_to_all | solution.py:575
  41.3 0.4 collective-permute-start.4
  41.6 3.1 %collective-permute-start.5 = (bf16[14,128,128]{2,1,0:T(8,128)(2,1)S(1)}, bf16[14,128,128]{2,1,0:T(8,128)(2,1)S(1)}, u32[]{:S(2)}, u32[]{:S(2)}) collective-permute-start(bf16[14,128,128]{2,1,0:T(8,128)(2,1)S(1)} %copy-done.28), channel_id=1, source_target_pairs={{0,16},{8,24},{16,0},{24,8},{1,17},{9,25},{17,1},{25,9},{2,18},{10... | collective-permute-start | bytes 1376264 | tf_op jit(solution)/shard_map/ppermute | solution.py:608
  44.7 7.7 %collective-permute-done.4.refs_0_ = bf16[14,128,128]{2,1,0:T(8,128)(2,1)S(1)} collective-permute-done((bf16[14,128,128]{2,1,0:T(8,128)(2,1)S(1)}, bf16[14,128,128]{2,1,0:T(8,128)(2,1)S(1)}, u32[]{:S(2)}, u32[]{:S(2)}) %collective-permute-start.4) | collective-permute-done | bytes 458784 | tf_op jit(solution)/shard_map/ppermute | solution.py:608
  52.4 21.1 %collective-permute-start.7 = (bf16[14,128,128]{2,1,0:T(8,128)(2,1)S(1)}, bf16[14,128,128]{2,1,0:T(8,128)(2,1)S(1)}, u32[]{:S(2)}, u32[]{:S(2)}) collective-permute-start(bf16[14,128,128]{2,1,0:T(8,128)(2,1)S(1)} %collective-permute-done.4.refs_0_), channel_id=1, source_target_pairs={{0,1},{1,0},{2,3},{3,2},{4,5},{5,4},{6,7},{7,6},{8,9},{9,8},{10,11... | collective-permute-start | bytes 1376264 | tf_op jit(solution)/shard_map/ppermute | solution.py:572
  73.5 6.4 %collective-permute-done.5.refs_1_ = bf16[14,128,128]{2,1,0:T(8,128)(2,1)S(1)} collective-permute-done((bf16[14,128,128]{2,1,0:T(8,128)(2,1)S(1)}, bf16[14,128,128]{2,1,0:T(8,128)(2,1)S(1)}, u32[]{:S(2)}, u32[]{:S(2)}) %collective-permute-start.5) | collective-permute-done | bytes 458784 | tf_op jit(solution)/shard_map/ppermute | solution.py:608
  79.9 2.0 %collective-permute-start.8 = (bf16[14,128,128]{2,1,0:T(8,128)(2,1)S(1)}, bf16[14,128,128]{2,1,0:T(8,128)(2,1)S(1)}, u32[]{:S(2)}, u32[]{:S(2)}) collective-permute-start(bf16[14,128,128]{2,1,0:T(8,128)(2,1)S(1)} %collective-permute-done.5.refs_1_), channel_id=1, source_target_pairs={{0,1},{1,0},{2,3},{3,2},{4,5},{5,4},{6,7},{7,6},{8,9},{9,8},{10,11... | collective-permute-start | bytes 1376264 | tf_op jit(solution)/shard_map/ppermute | solution.py:572
  81.9 1.9 %collective-permute-done.6.refs_2_ = bf16[14,128,128]{2,1,0:T(8,128)(2,1)S(1)} collective-permute-done((bf16[14,128,128]{2,1,0:T(8,128)(2,1)}, bf16[14,128,128]{2,1,0:T(8,128)(2,1)S(1)}, u32[]{:S(2)}, u32[]{:S(2)}) %collective-permute-start.6) | collective-permute-done | bytes 458784 | tf_op jit(solution)/shard_map/ppermute | solution.py:608
  83.8 1.2 collective-permute-start.9
  85.0 1.6 %collective-permute-done.9.refs_5_ = bf16[14,128,128]{2,1,0:T(8,128)(2,1)} collective-permute-done((bf16[14,128,128]{2,1,0:T(8,128)(2,1)S(1)}, bf16[14,128,128]{2,1,0:T(8,128)(2,1)}, u32[]{:S(2)}, u32[]{:S(2)}) %collective-permute-start.9) | collective-permute-done | bytes 458784 | tf_op jit(solution)/shard_map/ppermute | solution.py:572
  86.6 4.3 %pack_items.1 = (bf16[16,128,128]{2,1,0:T(8,128)(2,1)}, bf16[16,128,128]{2,1,0:T(8,128)(2,1)}, bf16[16,128,128]{2,1,0:T(8,128)(2,1)}, bf16[16,128,128]{2,1,0:T(8,128)(2,1)}) custom-call(s32[8,128]{1,0:T(8,128)} %copy-done.2, bf16[14,128,128]{2,1,0:T(8,128)(2,1)} %copy-done.20, bf16[14,128,128]{2,1,0:T(8,128)(2,1)} %copy-done.21, ...), custom_call_target="tpu_custom_call" | custom-call | tf_op jit(solution)/shard_map/pack_items/pallas_call | solution.py:289
  90.9 0.5 collective-permute-start.14
  91.4 1.2 collective-permute-start.10
  92.6 1.2 collective-permute-start.16
  93.8 0.3 collective-permute-start.18
  94.1 1.0 collective-permute-start.11
  95.0 3.2 %collective-permute-done.11 = f32[128,128]{1,0:T(8,128)S(1)} collective-permute-done((f32[128,128]{1,0:T(8,128)S(1)}, f32[128,128]{1,0:T(8,128)S(1)}, u32[]{:S(2)}, u32[]{:S(2)}) %collective-permute-start.11) | collective-permute-done | bytes 65568 | tf_op jit(solution)/shard_map/ppermute | solution.py:304
  98.3 0.1 collective-permute-start.12
  98.4 3.4 %collective-permute-done.12 = f32[128,128]{1,0:T(8,128)S(1)} collective-permute-done((f32[128,128]{1,0:T(8,128)S(1)}, f32[128,128]{1,0:T(8,128)S(1)}, u32[]{:S(2)}, u32[]{:S(2)}) %collective-permute-start.12) | collective-permute-done | bytes 65568 | tf_op jit(solution)/shard_map/ppermute | solution.py:304
  101.8 0.7 collective-permute-start.13
  102.5 3.7 %collective-permute-done.13 = f32[128,128]{1,0:T(8,128)S(1)} collective-permute-done((f32[128,128]{1,0:T(8,128)S(1)}, f32[128,128]{1,0:T(8,128)S(1)}, u32[]{:S(2)}, u32[]{:S(2)}) %collective-permute-start.13) | collective-permute-done | bytes 65568 | tf_op jit(solution)/shard_map/ppermute | solution.py:304
  106.2 2.1 %collective-permute-start.15 = (bf16[16,128,128]{2,1,0:T(8,128)(2,1)}, bf16[16,128,128]{2,1,0:T(8,128)(2,1)S(1)}, u32[]{:S(2)}, u32[]{:S(2)}) collective-permute-start(bf16[16,128,128]{2,1,0:T(8,128)(2,1)} %get-tuple-element.245.refs_2_), channel_id=1, source_target_pairs={{0,1},{1,0},{2,3},{3,2},{4,5},{5,4},{6,7},{7,6},{8,9},{9,8},{10,11... | collective-permute-start | bytes 1572872 | tf_op jit(solution)/shard_map/ppermute | solution.py:572
  108.3 0.1 collective-permute-start.20
  108.3 8.8 %collective-permute-done.16.refs_4_ = bf16[16,128,128]{2,1,0:T(8,128)(2,1)S(1)} collective-permute-done((bf16[16,128,128]{2,1,0:T(8,128)(2,1)}, bf16[16,128,128]{2,1,0:T(8,128)(2,1)S(1)}, u32[]{:S(2)}, u32[]{:S(2)}) %collective-permute-start.16) | collective-permute-done | bytes 524320 | tf_op jit(solution)/shard_map/ppermute | solution.py:626
  117.2 1.0 collective-permute-start.17
  118.1 0.6 slice.3
  119.4 0.3 collective-permute-done.17.refs_5_
  119.7 0.7 collective-permute-done.19.refs_7_
  120.4 1.0 copy-done.1
  121.5 17.3 %sweep.1 = f32[512,128]{1,0:T(8,128)} custom-call(s32[8,128]{1,0:T(8,128)S(1)} %copy-done.3, f32[512,128]{1,0:T(8,128)S(1)} %copy-done.14, f32[128,128]{1,0:T(8,128)S(1)} %add.205.gram_ref, bf16[128,128,128]{2,1,0:T(8,128)(2,1)} %all-to-all-done.3.refs_0_, bf16[128,128,128]{2,1,0:T(8,128)(2,1)S(1)} %collective-permute-done.14.refs_1_, ...), custom_call_target="tpu_custom_call" | custom-call | tf_op jit(solution)/shard_map/sweep/pallas_call | solution.py:249
  (50 shorter events, 0.1 us)
Async XLA Ops:
  6.5 4.1 %copy-start.5 = (bf16[4096,128]{1,0:T(8,128)(2,1)S(1)}, bf16[4096,128]{1,0:T(8,128)(2,1)}, u32[]{:S(2)}) copy-start(bf16[4096,128]{1,0:T(8,128)(2,1)} %param.18) | copy-start | bytes 3145732
  9.8 18.6 %copy-start = (bf16[64,128,128]{2,1,0:T(8,128)(2,1)}, bf16[64,128,128]{2,1,0:T(8,128)(2,1)S(1)}, u32[]{:S(2)}) copy-start(bf16[64,128,128]{2,1,0:T(8,128)(2,1)S(1)} %get-tuple-element.231.refs_2_) | copy-start | bytes 6291460
  9.8 1.8 %copy-start.26 = (s32[64]{0:T(128)S(1)}, s32[64]{0:T(128)}, u32[]{:S(2)}) copy-start(s32[64]{0:T(128)} %param.19) | copy-start | bytes 772
  9.9 1.8 %copy-start.27 = (s32[64]{0:T(128)S(1)}, s32[64]{0:T(128)}, u32[]{:S(2)}) copy-start(s32[64]{0:T(128)} %param.20) | copy-start | bytes 772
  9.9 18.6 %collective-permute-start.3 = (bf16[64,128,128]{2,1,0:T(8,128)(2,1)S(1)}, bf16[64,128,128]{2,1,0:T(8,128)(2,1)}, u32[]{:S(2)}, u32[]{:S(2)}) collective-permute-start(bf16[64,128,128]{2,1,0:T(8,128)(2,1)S(1)} %get-tuple-element.231.refs_2_), channel_id=1, source_target_pairs={{0,1},{1,0},{2,3},{3,2},{4,5},{5,4},{6,7},{7,6},{8,9},{9,8},{10,11... | collective-permute-start | bytes 6291464 | tf_op jit(solution)/shard_map/ppermute | solution.py:572
  10.6 17.9 %collective-permute-start.2 = (bf16[32,128,128]{2,1,0:T(8,128)(2,1)S(1)}, bf16[32,128,128]{2,1,0:T(8,128)(2,1)}, u32[]{:S(2)}, u32[]{:S(2)}) collective-permute-start(bf16[32,128,128]{2,1,0:T(8,128)(2,1)S(1)} %bitcast.109), channel_id=1, source_target_pairs={{0,1},{1,0},{2,3},{3,2},{4,5},{5,4},{6,7},{7,6},{8,9},{9,8},{10,11... | collective-permute-start | bytes 3145736 | tf_op jit(solution)/shard_map/ppermute | solution.py:572
  11.2 7.5 %collective-permute-start = (f32[128,128]{1,0:T(8,128)S(1)}, f32[128,128]{1,0:T(8,128)S(1)}, u32[]{:S(2)}, u32[]{:S(2)}) collective-permute-start(f32[128,128]{1,0:T(8,128)S(1)} %fusion.131), channel_id=1, source_target_pairs={{0,2},{1,3},{2,0},{3,1},{4,6},{5,7},{6,4},{7,5},{8,10},{9,11},{10,... | collective-permute-start | bytes 196616 | tf_op jit(solution)/shard_map/ppermute | solution.py:304
  12.3 11.1 %all-to-all-start.2 = ((s32[32,1,64]{2,1,0:T(1,128)}), s32[32,1,64]{2,1,0:T(1,128)S(1)}, u32[]{:S(2)}, u32[]{:S(2)}) async-start(s32[32,1,64]{2,1,0:T(1,128)} %broadcast_in_dim.41), calls=%async_computation.7 | async-start | bytes 32768 | tf_op jit(solution)/shard_map/all_to_all | solution.py:589
  18.7 9.1 %collective-permute-start.1 = (f32[128,128]{1,0:T(8,128)S(1)}, f32[128,128]{1,0:T(8,128)S(1)}, u32[]{:S(2)}, u32[]{:S(2)}) collective-permute-start(f32[128,128]{1,0:T(8,128)S(1)} %add.201), channel_id=1, source_target_pairs={{0,4},{1,5},{2,6},{3,7},{4,0},{5,1},{6,2},{7,3},{8,12},{9,13},{10,... | collective-permute-start | bytes 196616 | tf_op jit(solution)/shard_map/ppermute | solution.py:304
  27.2 0.6 copy-start.2
  35.2 6.1 %copy-start.29 = (bf16[14,128,128]{2,1,0:T(8,128)(2,1)S(1)}, bf16[14,128,128]{2,1,0:T(8,128)(2,1)}, u32[]{:S(2)}) copy-start(bf16[14,128,128]{2,1,0:T(8,128)(2,1)} %get-tuple-element.234) | copy-start | bytes 1376260
  35.2 6.4 %copy-start.28 = (bf16[14,128,128]{2,1,0:T(8,128)(2,1)S(1)}, bf16[14,128,128]{2,1,0:T(8,128)(2,1)}, u32[]{:S(2)}) copy-start(bf16[14,128,128]{2,1,0:T(8,128)(2,1)} %get-tuple-element.235) | copy-start | bytes 1376260
  35.2 55.7 %all-to-all-start.3 = ((bf16[128,128,128]{2,1,0:T(8,128)(2,1)}), bf16[128,128,128]{2,1,0:T(8,128)(2,1)}, u32[]{:S(2)}, u32[]{:S(2)}) async-start(bf16[128,128,128]{2,1,0:T(8,128)(2,1)} %get-tuple-element.232), calls=%async_computation.8 | async-start | bytes 8388608 | tf_op jit(solution)/shard_map/all_to_all | solution.py:575
  41.3 52.8 %copy-start.25 = (f32[128,128]{1,0:T(8,128)S(1)}, f32[128,128]{1,0:T(8,128)}, u32[]{:S(2)}) copy-start(f32[128,128]{1,0:T(8,128)} %add.202) | copy-start | bytes 196612
  41.3 76.9 %copy-start.3 = (s32[8,128]{1,0:T(8,128)S(1)}, s32[8,128]{1,0:T(8,128)}, u32[]{:S(2)}) copy-start(s32[8,128]{1,0:T(8,128)} %copy-done.2) | copy-start | bytes 12292
  41.3 79.1 %copy-start.14 = (f32[512,128]{1,0:T(8,128)S(1)}, f32[512,128]{1,0:T(8,128)}, u32[]{:S(2)}) copy-start(f32[512,128]{1,0:T(8,128)} %prior_ref.1) | copy-start | bytes 786436
  41.3 11.1 %collective-permute-start.4 = (bf16[14,128,128]{2,1,0:T(8,128)(2,1)S(1)}, bf16[14,128,128]{2,1,0:T(8,128)(2,1)S(1)}, u32[]{:S(2)}, u32[]{:S(2)}) collective-permute-start(bf16[14,128,128]{2,1,0:T(8,128)(2,1)S(1)} %copy-done.29), channel_id=1, source_target_pairs={{0,8},{8,16},{16,24},{24,0},{1,9},{9,17},{17,25},{25,1},{2,10},{10... | collective-permute-start | bytes 1376264 | tf_op jit(solution)/shard_map/ppermute | solution.py:608
  41.6 38.2 %collective-permute-start.5 = (bf16[14,128,128]{2,1,0:T(8,128)(2,1)S(1)}, bf16[14,128,128]{2,1,0:T(8,128)(2,1)S(1)}, u32[]{:S(2)}, u32[]{:S(2)}) collective-permute-start(bf16[14,128,128]{2,1,0:T(8,128)(2,1)S(1)} %copy-done.28), channel_id=1, source_target_pairs={{0,16},{8,24},{16,0},{24,8},{1,17},{9,25},{17,1},{25,9},{2,18},{10... | collective-permute-start | bytes 1376264 | tf_op jit(solution)/shard_map/ppermute | solution.py:608
  44.7 39.1 %collective-permute-start.6 = (bf16[14,128,128]{2,1,0:T(8,128)(2,1)}, bf16[14,128,128]{2,1,0:T(8,128)(2,1)S(1)}, u32[]{:S(2)}, u32[]{:S(2)}) collective-permute-start(bf16[14,128,128]{2,1,0:T(8,128)(2,1)} %get-tuple-element.236), channel_id=1, source_target_pairs={{0,24},{8,0},{16,8},{24,16},{1,25},{9,1},{17,9},{25,17},{2,26},{10... | collective-permute-start | bytes 1376264 | tf_op jit(solution)/shard_map/ppermute | solution.py:608
  52.4 34.2 %copy-start.20 = (bf16[14,128,128]{2,1,0:T(8,128)(2,1)}, bf16[14,128,128]{2,1,0:T(8,128)(2,1)S(1)}, u32[]{:S(2)}) copy-start(bf16[14,128,128]{2,1,0:T(8,128)(2,1)S(1)} %collective-permute-done.4.refs_0_) | copy-start | bytes 1376260
  52.4 32.6 %collective-permute-start.7 = (bf16[14,128,128]{2,1,0:T(8,128)(2,1)S(1)}, bf16[14,128,128]{2,1,0:T(8,128)(2,1)S(1)}, u32[]{:S(2)}, u32[]{:S(2)}) collective-permute-start(bf16[14,128,128]{2,1,0:T(8,128)(2,1)S(1)} %collective-permute-done.4.refs_0_), channel_id=1, source_target_pairs={{0,1},{1,0},{2,3},{3,2},{4,5},{5,4},{6,7},{7,6},{8,9},{9,8},{10,11... | collective-permute-start | bytes 1376264 | tf_op jit(solution)/shard_map/ppermute | solution.py:572
  79.9 6.7 %copy-start.21 = (bf16[14,128,128]{2,1,0:T(8,128)(2,1)}, bf16[14,128,128]{2,1,0:T(8,128)(2,1)S(1)}, u32[]{:S(2)}) copy-start(bf16[14,128,128]{2,1,0:T(8,128)(2,1)S(1)} %collective-permute-done.5.refs_1_) | copy-start | bytes 1376260
  79.9 5.1 %collective-permute-start.8 = (bf16[14,128,128]{2,1,0:T(8,128)(2,1)S(1)}, bf16[14,128,128]{2,1,0:T(8,128)(2,1)S(1)}, u32[]{:S(2)}, u32[]{:S(2)}) collective-permute-start(bf16[14,128,128]{2,1,0:T(8,128)(2,1)S(1)} %collective-permute-done.5.refs_1_), channel_id=1, source_target_pairs={{0,1},{1,0},{2,3},{3,2},{4,5},{5,4},{6,7},{7,6},{8,9},{9,8},{10,11... | collective-permute-start | bytes 1376264 | tf_op jit(solution)/shard_map/ppermute | solution.py:572
  83.8 2.8 %copy-start.22 = (bf16[14,128,128]{2,1,0:T(8,128)(2,1)}, bf16[14,128,128]{2,1,0:T(8,128)(2,1)S(1)}, u32[]{:S(2)}) copy-start(bf16[14,128,128]{2,1,0:T(8,128)(2,1)S(1)} %collective-permute-done.6.refs_2_) | copy-start | bytes 1376260
  83.8 2.8 %collective-permute-start.9 = (bf16[14,128,128]{2,1,0:T(8,128)(2,1)S(1)}, bf16[14,128,128]{2,1,0:T(8,128)(2,1)}, u32[]{:S(2)}, u32[]{:S(2)}) collective-permute-start(bf16[14,128,128]{2,1,0:T(8,128)(2,1)S(1)} %collective-permute-done.6.refs_2_), channel_id=1, source_target_pairs={{0,1},{1,0},{2,3},{3,2},{4,5},{5,4},{6,7},{7,6},{8,9},{9,8},{10,11... | collective-permute-start | bytes 1376264 | tf_op jit(solution)/shard_map/ppermute | solution.py:572
  85.0 1.6 %copy-start.23 = (bf16[14,128,128]{2,1,0:T(8,128)(2,1)}, bf16[14,128,128]{2,1,0:T(8,128)(2,1)S(1)}, u32[]{:S(2)}) copy-start(bf16[14,128,128]{2,1,0:T(8,128)(2,1)S(1)} %collective-permute-done.7.refs_3_) | copy-start | bytes 1376260
  85.0 1.6 %copy-start.24 = (bf16[14,128,128]{2,1,0:T(8,128)(2,1)}, bf16[14,128,128]{2,1,0:T(8,128)(2,1)S(1)}, u32[]{:S(2)}) copy-start(bf16[14,128,128]{2,1,0:T(8,128)(2,1)S(1)} %collective-permute-done.8.refs_4_) | copy-start | bytes 1376260
  90.9 29.5 %collective-permute-start.14 = (bf16[128,128,128]{2,1,0:T(8,128)(2,1)}, bf16[128,128,128]{2,1,0:T(8,128)(2,1)S(1)}, u32[]{:S(2)}, u32[]{:S(2)}) collective-permute-start(bf16[128,128,128]{2,1,0:T(8,128)(2,1)} %all-to-all-done.3.refs_0_), channel_id=1, source_target_pairs={{0,1},{1,0},{2,3},{3,2},{4,5},{5,4},{6,7},{7,6},{8,9},{9,8},{10,11... | collective-permute-start | bytes 12582920 | tf_op jit(solution)/shard_map/ppermute | solution.py:572
  91.4 16.9 %collective-permute-start.10 = (bf16[16,128,128]{2,1,0:T(8,128)(2,1)}, bf16[16,128,128]{2,1,0:T(8,128)(2,1)S(1)}, u32[]{:S(2)}, u32[]{:S(2)}) collective-permute-start(bf16[16,128,128]{2,1,0:T(8,128)(2,1)} %get-tuple-element.241), channel_id=1, source_target_pairs={{0,6},{1,7},{2,4},{3,5},{4,2},{5,3},{6,0},{7,1},{8,14},{9,15},{10,... | collective-permute-start | bytes 1572872 | tf_op jit(solution)/shard_map/ppermute | solution.py:626
  92.6 24.6 %collective-permute-start.16 = (bf16[16,128,128]{2,1,0:T(8,128)(2,1)}, bf16[16,128,128]{2,1,0:T(8,128)(2,1)S(1)}, u32[]{:S(2)}, u32[]{:S(2)}) collective-permute-start(bf16[16,128,128]{2,1,0:T(8,128)(2,1)} %get-tuple-element.246), channel_id=1, source_target_pairs={{0,2},{1,3},{2,0},{3,1},{4,6},{5,7},{6,4},{7,5},{8,10},{9,11},{10,... | collective-permute-start | bytes 1572872 | tf_op jit(solution)/shard_map/ppermute | solution.py:626
  93.8 24.4 %collective-permute-start.18 = (bf16[16,128,128]{2,1,0:T(8,128)(2,1)}, bf16[16,128,128]{2,1,0:T(8,128)(2,1)S(1)}, u32[]{:S(2)}, u32[]{:S(2)}) collective-permute-start(bf16[16,128,128]{2,1,0:T(8,128)(2,1)} %get-tuple-element.247), channel_id=1, source_target_pairs={{0,4},{1,5},{2,6},{3,7},{4,0},{5,1},{6,2},{7,3},{8,12},{9,13},{10,... | collective-permute-start | bytes 1572872 | tf_op jit(solution)/shard_map/ppermute | solution.py:626
  94.1 4.2 %collective-permute-start.11 = (f32[128,128]{1,0:T(8,128)S(1)}, f32[128,128]{1,0:T(8,128)S(1)}, u32[]{:S(2)}, u32[]{:S(2)}) collective-permute-start(f32[128,128]{1,0:T(8,128)S(1)} %copy-done.25), channel_id=1, source_target_pairs={{0,1},{1,0},{2,3},{3,2},{4,5},{5,4},{6,7},{7,6},{8,9},{9,8},{10,11... | collective-permute-start | bytes 196616 | tf_op jit(solution)/shard_map/ppermute | solution.py:304
  98.3 3.5 %collective-permute-start.12 = (f32[128,128]{1,0:T(8,128)S(1)}, f32[128,128]{1,0:T(8,128)S(1)}, u32[]{:S(2)}, u32[]{:S(2)}) collective-permute-start(f32[128,128]{1,0:T(8,128)S(1)} %add.203), channel_id=1, source_target_pairs={{0,8},{8,0},{16,24},{24,16},{1,9},{9,1},{17,25},{25,17},{2,10},{10... | collective-permute-start | bytes 196616 | tf_op jit(solution)/shard_map/ppermute | solution.py:304
  101.8 4.4 %collective-permute-start.13 = (f32[128,128]{1,0:T(8,128)S(1)}, f32[128,128]{1,0:T(8,128)S(1)}, u32[]{:S(2)}, u32[]{:S(2)}) collective-permute-start(f32[128,128]{1,0:T(8,128)S(1)} %add.204), channel_id=1, source_target_pairs={{0,16},{8,24},{16,0},{24,8},{1,17},{9,25},{17,1},{25,9},{2,18},{10... | collective-permute-start | bytes 196616 | tf_op jit(solution)/shard_map/ppermute | solution.py:304
  106.2 13.2 %collective-permute-start.15 = (bf16[16,128,128]{2,1,0:T(8,128)(2,1)}, bf16[16,128,128]{2,1,0:T(8,128)(2,1)S(1)}, u32[]{:S(2)}, u32[]{:S(2)}) collective-permute-start(bf16[16,128,128]{2,1,0:T(8,128)(2,1)} %get-tuple-element.245.refs_2_), channel_id=1, source_target_pairs={{0,1},{1,0},{2,3},{3,2},{4,5},{5,4},{6,7},{7,6},{8,9},{9,8},{10,11... | collective-permute-start | bytes 1572872 | tf_op jit(solution)/shard_map/ppermute | solution.py:572
  108.3 11.1 %collective-permute-start.20 = (bf16[16,128,128]{2,1,0:T(8,128)(2,1)S(1)}, bf16[16,128,128]{2,1,0:T(8,128)(2,1)S(1)}, u32[]{:S(2)}, u32[]{:S(2)}) collective-permute-start(bf16[16,128,128]{2,1,0:T(8,128)(2,1)S(1)} %collective-permute-done.10.refs_8_), channel_id=1, source_target_pairs={{0,1},{1,0},{2,3},{3,2},{4,5},{5,4},{6,7},{7,6},{8,9},{9,8},{10,11... | collective-permute-start | bytes 1572872 | tf_op jit(solution)/shard_map/ppermute | solution.py:572
  117.2 2.5 %collective-permute-start.17 = (bf16[16,128,128]{2,1,0:T(8,128)(2,1)S(1)}, bf16[16,128,128]{2,1,0:T(8,128)(2,1)S(1)}, u32[]{:S(2)}, u32[]{:S(2)}) collective-permute-start(bf16[16,128,128]{2,1,0:T(8,128)(2,1)S(1)} %collective-permute-done.16.refs_4_), channel_id=1, source_target_pairs={{0,1},{1,0},{2,3},{3,2},{4,5},{5,4},{6,7},{7,6},{8,9},{9,8},{10,11... | collective-permute-start | bytes 1572872 | tf_op jit(solution)/shard_map/ppermute | solution.py:572
  118.1 2.3 %collective-permute-start.19 = (bf16[16,128,128]{2,1,0:T(8,128)(2,1)S(1)}, bf16[16,128,128]{2,1,0:T(8,128)(2,1)S(1)}, u32[]{:S(2)}, u32[]{:S(2)}) collective-permute-start(bf16[16,128,128]{2,1,0:T(8,128)(2,1)S(1)} %collective-permute-done.18.refs_6_), channel_id=1, source_target_pairs={{0,1},{1,0},{2,3},{3,2},{4,5},{5,4},{6,7},{7,6},{8,9},{9,8},{10,11... | collective-permute-start | bytes 1572872 | tf_op jit(solution)/shard_map/ppermute | solution.py:572
  120.4 1.0 copy-start.1
